TPU v7x, 32 devices: a whole 2x2x4 slice. The times are simulated.
32 devices in a mesh: dp: 16 (over z, y, x), mp: 2 (over core).
Axes of the slice: x: 2, y: 2, z: 4, core: 2. Of those that a mesh axis runs over, the one named last changes fastest.
Arguments:
- x_short: bfloat16 [64, 256, 768], P('dp'), may hold values from -6 to 6
- x_long: bfloat16 [32, 512, 768], P('dp'), may hold values from -6 to 6
- len_short: int32 [64], P('dp'), may hold values from 64 to 256, as said below
- len_long: int32 [32], P('dp'), may hold values from 128 to 512, as said below
- boundaries: int32 [15], replicated, may hold values from 1 to 128, as said below
- q_weight: bfloat16 [768, 768], P('dp', 'mp'), may hold values from -0.109375 to 0.109375
- k_weight: bfloat16 [768, 768], P('dp', 'mp'), may hold values from -0.109375 to 0.109375
- v_weight: bfloat16 [768, 768], P('dp', 'mp'), may hold values from -0.21875 to 0.21875
- out_weight: bfloat16 [768, 768], P('dp', 'mp'), may hold values from -0.625 to 0.625
- in_weight: bfloat16 [768, 3072], P('dp', 'mp'), may hold values from -0.21875 to 0.21875
- ff_out_weight: bfloat16 [768, 3072], P('dp', 'mp'), may hold values from -0.15625 to 0.15625
- attn_gain: bfloat16 [768], P('dp'), may hold values from 0.5 to 1.5
- ffn_gain: bfloat16 [768], P('dp'), may hold values from 0.5 to 1.5
- bias_table: bfloat16 [32, 12], P(None, 'mp'), may hold values from -4 to 4
- cot_short: bfloat16 [64, 256, 768], P('dp'), may hold values from -6 to 6
- cot_long: bfloat16 [32, 512, 768], P('dp'), may hold values from -6 to 6
Outputs:
- out_short: bfloat16 [64, 256, 768], P('dp')
- out_long: bfloat16 [32, 512, 768], P('dp')
- grad_short: bfloat16 [64, 256, 768], P('dp')
- grad_long: bfloat16 [32, 512, 768], P('dp')
- grad_q_weight: float32 [768, 768], P('dp', 'mp')
- grad_k_weight: float32 [768, 768], P('dp', 'mp')
- grad_v_weight: float32 [768, 768], P('dp', 'mp')
- grad_out_weight: float32 [768, 768], P('dp', 'mp')
- grad_in_weight: float32 [768, 3072], P('dp', 'mp')
- grad_ff_out_weight: float32 [768, 3072], P('dp', 'mp')
- grad_attn_gain: float32 [768], P('dp')
- grad_ffn_gain: float32 [768], P('dp')
- grad_bias_table: float32 [32, 12], P(None, 'mp')
Inputs may be any that keep to these rules, and one draw needn't show every extreme that they name: `len_short`: valid positions at the head of each slot of 256; the rest is padding. `len_long`: valid positions at the head of each slot of 512; the rest is padding. `boundaries`: strictly increasing thresholds on the distance; the first is 1 and the last 128.
All inputs are finite; a program needn't handle non-finite values.
Results may differ from a plain program's by a relative error of at most 0.02.
Values may be sent and summed in bfloat16 or wider, within the bound.
No kernel may reach another device: no remote copies, remote signals or barrier semaphores. Data moves between devices by JAX's collectives and lax.ppermute only.
A program may use at most 192 MiB of HBM per device.

v0:
```python
import functools

import jax
import jax.numpy as jnp
from jax import lax
from jax.experimental import pallas as pl
from jax.experimental.pallas import tpu as pltpu
from jax.sharding import PartitionSpec as P

DH = 64
LANES = 128
EPS = 1e-06
NEG = -1000000000.0
BF = jnp.bfloat16
F32 = jnp.float32
ANY = pl.BlockSpec(memory_space=pl.ANY)
HBM = pl.BlockSpec(memory_space=pltpu.HBM)
SMEM = pl.BlockSpec(memory_space=pltpu.SMEM)
VMEM = pl.BlockSpec(memory_space=pltpu.VMEM)


def dot(left, right):
    return jnp.dot(left, right, preferred_element_type=F32)


def dot_rows(left, right):
    return lax.dot_general(left, right, (((0,), (0,)), ((), ())), preferred_element_type=F32)


def dot_cols(left, right):
    return lax.dot_general(left, right, (((1,), (1,)), ((), ())), preferred_element_type=F32)


def tiles(array, rows):
    return pl.BlockSpec((rows,) + array.shape[1:], lambda i: (i,) + (0,) * (len(array.shape) - 1))


def fixed(array):
    return pl.BlockSpec(array.shape, lambda i: (0,) * len(array.shape))


def pair_tiles(pair, rows):
    count = pair[0].shape[0] // rows
    rest = (0,) * (pair[0].ndim - 1)
    shape = (rows,) + pair[0].shape[1:]
    return [
        pl.BlockSpec(shape, lambda i: (jnp.minimum(i, count - 1),) + rest),
        pl.BlockSpec(shape, lambda i: (jnp.maximum(i - count, 0),) + rest),
    ]


def pick(count, first, second):
    return jnp.where(pl.program_id(0) < count, first[...], second[...])


def out_of(shape, kind):
    return jax.ShapeDtypeStruct(tuple(shape), kind)


def call(kernel, outs, args, *, ins=None, out_specs=None, grid=None, scratch=(), us=0.001, mib=4, after=(), through=()):
    ins = list(ins or [VMEM] * len(args))
    out_specs = list(out_specs or [VMEM] * len(outs))
    extra = {} if grid is None else {"grid": grid}
    idle = len(after) + len(through)

    def body(*refs):
        given, made = refs[: len(args)], refs[len(args) + idle :]
        kernel(*given, *made[: len(outs)], *made[len(outs) + len(through) :])

    return pl.pallas_call(
        body,
        out_shape=list(outs) + [out_of(t.shape, t.dtype) for t in through],
        in_specs=ins + [ANY] * idle,
        out_specs=out_specs + [ANY] * len(through),
        scratch_shapes=list(scratch),
        compiler_params=pltpu.CompilerParams(vmem_limit_bytes=mib << 20),
        input_output_aliases={len(args) + len(after) + i: len(outs) + i for i in range(len(through))},
        cost_estimate=pl.CostEstimate(flops=int(us * 1e9), bytes_accessed=1000, transcendentals=0),
        **extra,
    )(*args, *after, *through)


class Ring:
    def __init__(self, sizes):
        self.dp, self.mp = sizes
        self.me = lax.axis_index("dp")
        self.odd = lax.axis_index("mp") & 1
        self.quarter = self.dp // 4
        j = jnp.arange(self.dp, dtype=jnp.int32)
        first = (j // self.quarter) & 1
        last = j // (2 * self.quarter)

        def order(odd):
            low = jnp.where(odd == 0, first + 2 * last, 2 * first + last)
            return self.me ^ (4 * (j % self.quarter) + low)

        self.order = order(self.odd)
        self.orders = [order(self.odd ^ (k & 1)) for k in range(1, self.mp)]
        rel = self.me ^ j
        bit0, bit1 = rel & 1, (rel >> 1) & 1
        first, last = jnp.where(self.odd == 0, bit0, bit1), jnp.where(self.odd == 0, bit1, bit0)
        self.spots = (rel >> 2) + self.quarter * (first + 2 * last)
        lead = (lax.axis_index("mp") == 0).astype(jnp.int32)
        self.places = jnp.concatenate([self.order, lead[None]])

    def far(self, array):
        return [
            lax.ppermute(array, "dp", [(i, i ^ (4 * step)) for i in range(self.dp)])
            for step in range(1, self.quarter)
        ]

    def far_all(self, arrays):
        return [
            lax.ppermute(a, "dp", [(i, i ^ (4 * (step + 1))) for i in range(self.dp)])
            for step, a in enumerate(arrays)
        ]

    def near(self, array, masks):
        pairs = [
            (i * self.mp + c, (i ^ masks[c & 1]) * self.mp + c)
            for i in range(self.dp)
            for c in range(self.mp)
        ]
        return lax.ppermute(array, ("dp", "mp"), pairs)

    def first(self, array):
        return self.near(array, (1, 2))

    def last(self, array):
        return self.near(array, (2, 1))

    def exchange(self, array):
        return [
            lax.ppermute(array, "mp", [(i, i ^ k) for i in range(self.mp)])
            for k in range(1, self.mp)
        ]


def join_kernel(plan, *refs):
    sources, outs = refs[: -len(plan)], refs[-len(plan) :]
    for (chosen, start, stop), out in zip(plan, outs):
        at = 0
        for i in chosen:
            count = sources[i].shape[0]
            out[at : at + count] = sources[i][:, :, start:stop]
            at += count


def join(arrays, plan, after=(), through=()):
    outs = []
    for chosen, start, stop in plan:
        count = sum(arrays[i].shape[0] for i in chosen)
        outs.append(out_of((count, arrays[0].shape[1], stop - start), arrays[0].dtype))
    return call(functools.partial(join_kernel, plan), outs, arrays, after=after, through=through)


def aligned(rows):
    return rows % 16 == 0


def blocks_of(ring, held, got):
    if aligned(held.shape[1]):
        return (held, got)
    blocks = jnp.take(jnp.concatenate([held, got], 0), ring.spots, axis=0)
    return (blocks.reshape((-1,) + held.shape[2:]),)


def load(places, sources, to, at):
    there = slice(at, at + sources[0].shape[-1])
    if len(sources) == 2:
        half, rows, _ = sources[0].shape
        for j in range(2 * half):
            row = pl.multiple_of(places[j] * rows, 16)
            to[pl.ds(row, rows), there] = sources[j // half][j % half]
    else:
        to[:, there] = sources[0][...]
    return there.stop


def columns(array, at, count):
    first = (0,) * (array.ndim - 1)
    return pl.BlockSpec(
        array.shape[:-1] + (count,),
        lambda i: first + (at // count,),
        pipeline_mode=pl.Buffered(1),
    )


def emit(places, total, keep, send, extra=None):
    half, rows, _ = keep.shape
    for j in range(2 * half):
        at = pl.multiple_of(places[j] * rows, 16)
        block = total[pl.ds(at, rows), :]
        if extra is not None:
            block = block + extra
        if j < half:
            keep[j] = block
        else:
            send[j - half] = block.astype(BF)


def emitted(ring, rows, cols):
    share = rows // ring.dp
    if aligned(share):
        shape = (ring.dp // 2, share, cols)
        return [out_of(shape, F32), out_of(shape, BF)]
    return [out_of((rows, cols), F32)]


def halves(ring, outs, extra=None):
    if len(outs) == 2:
        return outs
    blocks = outs[0].reshape(ring.dp, -1, outs[0].shape[1])
    if extra is not None:
        blocks = blocks + extra
    blocks = jnp.take(blocks, ring.order, axis=0)
    return blocks[: ring.dp // 2], blocks[ring.dp // 2 :].astype(BF)


def fold_kernel(modes, *refs):
    ins, outs = refs[: 2 * len(modes)], refs[2 * len(modes) :]
    for mode in modes:
        keep, got = ins[:2]
        ins = ins[2:]
        count = got.shape[0] if mode else got.shape[0] // 2
        if mode:
            outs[0][...] = keep[0] + got[0].astype(F32)
            for j in range(1, count):
                outs[j][...] = (keep[j] + got[j].astype(F32)).astype(BF)
            outs = outs[count:]
        else:
            outs[0][...] = keep[:count] + got[:count].astype(F32)
            outs[1][...] = (keep[count:] + got[count:].astype(F32)).astype(BF)
            outs = outs[2:]


def fold(*items, after=(), through=()):
    outs = []
    args = []
    for keep, got, mode in items:
        args += [keep, got]
        if mode:
            shape = keep.shape[1:]
            outs += [out_of(shape, F32)] + [out_of(shape, BF)] * (keep.shape[0] - 1)
        else:
            shape = (keep.shape[0] // 2,) + keep.shape[1:]
            outs += [out_of(shape, F32), out_of(shape, BF)]
    kernel = functools.partial(fold_kernel, [m for *_, m in items])
    return call(kernel, outs, args, after=after, through=through)


def final_kernel(counts, plan, scaled, carried, gain_ref, *refs):
    carry, refs = refs[:carried], refs[carried:]
    weights, refs = refs[: len(scaled)], refs[len(scaled) :]
    fields = []
    for count in counts:
        total = refs[0][...]
        for r in refs[1:count]:
            total = total + r[...].astype(F32)
        fields.append(total)
        refs = refs[count:]
    outs, gain_out = refs[:-1], refs[-1]
    sums = jnp.zeros(gain_out.shape, F32)
    for i, (out, spans) in enumerate(zip(outs, plan)):
        at = 0
        for f, start, stop in spans:
            value = fields[f][:, start:stop]
            there = slice(at, at + stop - start)
            if i in scaled:
                kept = weights[scaled.index(i)][:, there].astype(F32)
                sums += jnp.sum(value * kept, 1, keepdims=True)
                value = value * gain_ref[...]
            out[:, there] = value
            at += stop - start
    if carried:
        lane = lax.broadcasted_iota(jnp.int32, sums.shape, 1)
        sums = jnp.where(lane == 0, sums, carry[0][...])
    gain_out[...] = sums


def final(items, plan, scaled, gain, weights, carry=(), after=()):
    rows = gain.shape[0]
    outs = [out_of((rows, sum(b - a for _, a, b in spans)), F32) for spans in plan]
    outs.append(out_of((rows, LANES), F32))
    kernel = functools.partial(final_kernel, [len(i) for i in items], plan, scaled, len(carry))
    args = [gain, *carry, *weights, *[a for i in items for a in i]]
    return call(kernel, outs, args, after=after)


def distance_buckets(bounds_ref, dist, buckets):
    size = jnp.abs(dist)
    half = jnp.zeros(dist.shape, jnp.int32)
    for b in range(bounds_ref.shape[0]):
        half += (size >= bounds_ref[b]).astype(jnp.int32)
    return half + jnp.where(dist > 0, buckets // 2, 0)


def bases_kernel(bounds_ref, table_ref, near_ref, far_ref):
    heads, _, width = near_ref.shape
    buckets = table_ref.shape[1]
    row = lax.broadcasted_iota(jnp.int32, (8, width), 0)
    for to, sign in ((near_ref, 1), (far_ref, -1)):
        dist = sign * (lax.broadcasted_iota(jnp.int32, (8, width), 1) - width // 2)
        marks = distance_buckets(bounds_ref, dist, buckets)
        marks = jnp.concatenate([marks] * (buckets // 8), 0)
        onehot = (marks == lax.broadcasted_iota(jnp.int32, (buckets, width), 0)).astype(F32)
        line = dot(table_ref[...], onehot.astype(BF))
        for h in range(heads):
            field = jnp.broadcast_to(line[h : h + 1], (8, width))
            for k in (1, 2, 4):
                field = jnp.where((row & k) != 0, pltpu.roll(field, k, 1), field)
            while field.shape[0] < LANES:
                field = jnp.concatenate([field, pltpu.roll(field, field.shape[0], 1)], 0)
            to[h] = field


def bias_bases(boundaries, table, heads, width, after=()):
    shape = out_of((heads, LANES, width), F32)
    return call(
        bases_kernel, [shape, shape], [boundaries, table], ins=[SMEM, VMEM], mib=16, after=after
    )


def bucket_field(bounds_ref, fields, buckets, first):
    width = fields[0].shape[-1]
    dist = width // 2 - lax.broadcasted_iota(jnp.int32, (8, width), 1)
    marks = distance_buckets(bounds_ref, dist, buckets)
    row = lax.broadcasted_iota(jnp.int32, (8, width), 0)
    line = jnp.zeros((8, width), F32)
    for h, field in enumerate(fields, first):
        while field.shape[0] > 8:
            half = field.shape[0] // 2
            field = field[:half] + pltpu.roll(field[half:], width - half, 1)
        for k in (4, 2, 1):
            field = jnp.where((row & k) != 0, pltpu.roll(field, width - k, 1), field)
        line = jnp.where(row == h, jnp.sum(field, 0, keepdims=True), line)
    lane = lax.broadcasted_iota(jnp.int32, (8, LANES), 1)
    out = jnp.zeros((8, LANES), F32)
    for b in range(buckets):
        total = jnp.sum(jnp.where(marks == b, line, 0.0), 1, keepdims=True)
        out = jnp.where(lane == b, total, out)
    return out


def split_low(values, lane, off, rest):
    high = values.astype(BF).astype(F32)
    mid = (values - high).astype(BF).astype(F32)
    low = values - high - mid
    return jnp.where(
        lane == off,
        high,
        jnp.where(lane == off + 1, mid, jnp.where(lane == off + 2, low, rest)),
    )


def three_ones(lane, off):
    return jnp.where((lane >= off) & (lane < off + 3), 1.0, 0.0)


def slots_of(batches):
    at = 0
    for b, (slots, length) in enumerate(batches):
        for s in range(slots):
            yield b, s, length, slice(at, at + length)
            at += length


def attend_kernel(batches, halves, *refs):
    places, lens = refs[0], refs[1 : 1 + len(batches)]
    refs = refs[1 + len(batches) :]
    normed_ref, near_ref = refs[:2]
    sources = refs[2 : 2 + halves]
    aug_ref, k_ref, v_ref, o_ref, w_scr = refs[2 + halves :]
    width = near_ref.shape[-1]
    load(places, sources, w_scr, 0)
    for b, s, length, span in slots_of(batches):
        valid = lens[b][s]
        lane = lax.broadcasted_iota(jnp.int32, (length, LANES), 1)
        place = lax.broadcasted_iota(jnp.int32, (length, LANES), 0)
        masked = jnp.where(place >= valid, NEG, 0.0)
        qkv = dot(normed_ref[span, :], w_scr[...])
        q, k, v = (qkv[:, i * LANES : (i + 1) * LANES] for i in range(3))
        k_ref[span, :] = k.astype(BF)
        v_ref[span, :] = v.astype(BF)
        mixed = []
        for e in range(2):
            own = (lane >= DH) == (e == 1)
            off = DH * (1 - e)
            marker = jnp.where(lane == off + 3, 1.0, 0.0)
            q_own = jnp.where(own, q, marker).astype(BF)
            k_own = jnp.where(own, k, jnp.where(lane == off + 3, masked, 0.0)).astype(BF)
            v_own = jnp.where(own, v, 1.0).astype(BF)
            start = width // 2
            bias = [
                near_ref[e, :, start - a * LANES : start - a * LANES + length]
                for a in range(length // LANES)
            ]
            scores = dot_cols(q_own, k_own) + jnp.concatenate(bias, 0)
            top = jnp.max(scores, 1, keepdims=True)
            expo = jnp.exp(scores - top)
            sums = dot(expo.astype(BF), v_own)
            total = jnp.where(own, pltpu.roll(sums, DH, 1), sums)
            logsum = top + jnp.log(total)
            extra = split_low(-logsum, lane, off, marker)
            aug_ref[span, e * LANES : (e + 1) * LANES] = jnp.where(own, q, extra).astype(BF)
            mixed.append(sums / total)
        o_ref[span, :] = jnp.where(lane < DH, mixed[0], mixed[1]).astype(BF)


def pair_of(base, pair):
    return pl.BlockSpec((2,) + base.shape[1:], lambda i: (pair, 0, 0))


def attend(ring, batches, lens, near, unit, weights, at, pair, after=()):
    rows, width = unit.shape
    shapes = [out_of((rows, c * LANES), BF) for c in (2, 1, 1, 1)]
    return call(
        functools.partial(attend_kernel, batches, len(weights)),
        shapes,
        [ring.places, *lens, unit, near, *weights],
        ins=[SMEM] * (1 + len(lens))
        + [fixed(unit), pair_of(near, pair)]
        + [columns(w, at, 3 * LANES) for w in weights],
        out_specs=[fixed(s) for s in shapes],
        grid=(1,),
        scratch=[pltpu.VMEM((width, 3 * LANES), BF)],
        mib=16,
        after=after,
    )


def attend_back_kernel(batches, pair, buckets, before, priors, emits, *refs):
    lens, refs = refs[: len(batches)], refs[len(batches) :]
    bounds, places, unit_ref, go_ref, aug_ref, k_ref, v_ref, o_ref, far_ref = refs[:9]
    totals, (table_in, grads_ref, table_ref) = refs[9 : 9 + priors], refs[9 + priors : 12 + priors]
    outs, (gbase_ref, total) = refs[12 + priors : -2], refs[-2:]
    width = far_ref.shape[-1]
    gbase_ref[...] = jnp.zeros_like(gbase_ref)
    for b, s, length, span in slots_of(batches):
        valid = lens[b][s]
        lane = lax.broadcasted_iota(jnp.int32, (length, LANES), 1)
        place = lax.broadcasted_iota(jnp.int32, (length, LANES), 0)
        masked = jnp.where(place >= valid, NEG, 0.0)
        k = k_ref[span, :].astype(F32)
        v = v_ref[span, :].astype(F32)
        go = go_ref[span, :].astype(F32)
        both = go * o_ref[span, :].astype(F32)
        grads = []
        for e in range(2):
            own = (lane >= DH) == (e == 1)
            off = DH * (1 - e)
            q_own = aug_ref[span, e * LANES : (e + 1) * LANES]
            ones = three_ones(lane, off)
            k_own = jnp.where(own, k, jnp.where(lane == off + 3, masked, ones)).astype(BF)
            v_own = jnp.where(own, v, ones).astype(BF)
            delta = jnp.sum(jnp.where(own, both, 0.0), 1, keepdims=True)
            g_own = jnp.where(own, go, split_low(-delta, lane, off, 0.0)).astype(BF)
            cols = [
                slice(width // 2 - a * LANES, width // 2 - a * LANES + length)
                for a in range(length // LANES)
            ]
            bias = jnp.concatenate([far_ref[e, :, c] for c in cols], 0)
            probs = jnp.exp(dot_cols(k_own, q_own) + bias)
            ds = probs * dot_cols(v_own, g_own)
            for a, c in enumerate(cols):
                gbase_ref[e, :, c] += ds[a * LANES : (a + 1) * LANES]
            ds = ds.astype(BF)
            gv = dot(probs.astype(BF), g_own)
            grads.append((dot_rows(ds, k_own), dot(ds, q_own), gv))
        first = lane < DH
        for i, (a, b) in enumerate(zip(*grads)):
            grads_ref[span, i * LANES : (i + 1) * LANES] = jnp.where(first, a, b).astype(BF)
    table = table_in[...] + bucket_field(
        bounds, [gbase_ref[0], gbase_ref[1]], buckets, 2 * pair
    )
    table_ref[...] = table
    part = dot_rows(unit_ref[...], grads_ref[...])
    if not emits:
        outs[0][...] = part
        return
    step = 3 * LANES
    at = 0
    for value in [r[...] for r in totals[:before]] + [part] + [r[...] for r in totals[before:]]:
        total[:, at : at + value.shape[1]] = value
        at += value.shape[1]
    extra = None
    if total.shape[1] > at:
        total[:, at:] = jnp.zeros((total.shape[0], LANES), F32)
    if total.shape[1] > at and emits == 2:
        rows = outs[0].shape[1]
        extra = jnp.concatenate([table, jnp.zeros((rows - 8, LANES), F32)], 0)
        extra = jnp.concatenate([jnp.zeros((rows, at), F32), extra], 1)
    if emits == 2:
        emit(places, total, *outs, extra=extra)
    else:
        outs[0][...] = total[...]


def attend_back(
    ring, batches, lens, boundaries, buckets, far, unit, go, fwd, pair, table, before, rest, last, after=()
):
    rows, width = unit.shape
    step = 3 * LANES
    go_spec = pl.BlockSpec((rows, LANES), lambda i: (0, pair))
    given = rest is None
    priors = [] if given else [*before, *rest]
    cols = step + sum(p.shape[1] for p in priors) + (LANES if last else 0)
    outs = [out_of((rows, step), BF), out_of((8, LANES), F32)]
    made = [out_of((width, step), F32)] if given else emitted(ring, width, cols)
    emits = 0 if given else len(made)
    kernel = functools.partial(
        attend_back_kernel, batches, pair, buckets, len(before), len(priors), emits
    )
    grads, table, *made = call(
        kernel,
        outs + made,
        [*lens, boundaries, ring.places, unit, go, *fwd, far, *priors, table],
        ins=[SMEM] * (len(lens) + 2)
        + [fixed(unit), go_spec]
        + [fixed(a) for a in fwd]
        + [pair_of(far, pair)]
        + [fixed(a) for a in (*priors, table)],
        out_specs=[fixed(o) for o in outs + made],
        grid=(1,),
        scratch=[
            pltpu.VMEM((2,) + far.shape[1:], F32),
            pltpu.VMEM((8, LANES) if given else (width, cols), F32),
        ],
        mib=24,
        after=after,
    )
    if not given:
        share = width // ring.dp
        extra = jnp.pad(table, ((0, share - 8), (cols - LANES, 0))) if last else None
        made = halves(ring, made, extra)
    return grads, table, made


def rms_parts(field):
    scale = lax.rsqrt(jnp.mean(field * field, -1, keepdims=True) + EPS)
    return (scale, field * scale)


def norm_back(grad_unit, unit, scale):
    return scale * (grad_unit - unit * jnp.mean(grad_unit * unit, -1, keepdims=True))


def norm_kernel(count, short_ref, long_ref, unit_ref):
    unit_ref[...] = rms_parts(pick(count, short_ref, long_ref).astype(F32))[1].astype(BF)


def norm(xs, tile=512, after=()):
    out = out_of((xs[0].shape[0] + xs[1].shape[0], xs[0].shape[1]), BF)
    return call(
        functools.partial(norm_kernel, xs[0].shape[0] // tile),
        [out],
        xs,
        ins=pair_tiles(xs, tile),
        out_specs=[tiles(out, tile)],
        grid=(out.shape[0] // tile,),
        mib=8,
        after=after,
    )[0]


def sum_of(refs):
    total = refs[0][...].astype(F32)
    for r in refs[1:]:
        total = total + r[...].astype(F32)
    return total


def add_kernel(count, addends, *refs):
    value = sum_of(refs[:addends]).astype(BF)

    @pl.when(pl.program_id(0) < count)
    def _():
        refs[-2][...] = value

    @pl.when(pl.program_id(0) >= count)
    def _():
        refs[-1][...] = value


def add_all(shapes, fields, tile=512, after=()):
    outs = [out_of(s, BF) for s in shapes]
    return call(
        functools.partial(add_kernel, shapes[0][0] // tile, len(fields)),
        outs,
        fields,
        ins=[tiles(f, tile) for f in fields],
        out_specs=pair_tiles(outs, tile),
        grid=((shapes[0][0] + shapes[1][0]) // tile,),
        after=after,
    )


def gelu_parts(x):
    c = 0.7978845608028654
    d = c * 0.044715
    square = x * x
    t = jnp.tanh(x * (c + d * square))
    half = 0.5 + 0.5 * t
    slope = half + (0.5 * x) * (1.0 - t * t) * (c + 3.0 * d * square)
    return x * half, slope


def ffn_first_kernel(halves, groups, pairs, emits, count, places, *refs):
    all_places, refs = [places, places, *refs[: groups - 1]], refs[groups - 1 :]
    g_refs, x_refs, refs = refs[:2], refs[2:4], refs[4:]
    o_refs, refs = refs[: groups * pairs], refs[groups * pairs :]
    sources, refs = refs[:halves], refs[halves:]
    unit_ref, scale_ref, out_ref, gn_ref = refs[:4]
    grads, (w_scr, total) = refs[4 : 4 + emits], refs[4 + emits :]
    units = total.shape[1] // 2
    step = pl.program_id(0)

    @pl.when(step == 0)
    def _():
        total[...] = jnp.zeros_like(total)
        at = 0
        count = halves // (1 + groups)
        for i, there in enumerate(all_places):
            at = load(there, sources[i * count : (i + 1) * count], w_scr, at)

    mixed = jnp.concatenate([r[...] for r in o_refs], 1)
    middle = pick(count, *x_refs).astype(F32) + dot_cols(mixed, w_scr[:, 2 * units :])
    scale, unit = rms_parts(middle)
    unit = unit.astype(BF)
    unit_ref[...] = unit
    scale_ref[...] = jnp.broadcast_to(scale, scale_ref.shape)
    g = pick(count, *g_refs)
    win, wout = w_scr[:, :units], w_scr[:, units : 2 * units]
    act, slope = gelu_parts(dot(unit, win))
    act = act.astype(BF)
    gpre = (dot(g, wout) * slope).astype(BF)
    lead = places[places.shape[0] - 1].astype(F32)
    out_ref[...] = (dot_cols(act, wout) + lead * middle).astype(BF)
    gn_ref[...] = dot_cols(gpre, win).astype(BF)
    total[:, :units] += dot_rows(unit, gpre)
    total[:, units:] += dot_rows(g, act)

    @pl.when(step == pl.num_programs(0) - 1)
    def _():
        if emits == 2:
            emit(places, total, *grads)
        else:
            grads[0][...] = total[...]


def ffn_first(ring, gs, xs, mixed, weights, out_weights, units, tile=512, after=()):
    rows = mixed[0].shape[0]
    width = xs[0].shape[1]
    groups = len(out_weights)
    pairs = len(mixed) // groups
    field = out_of((rows, width), BF)
    outs = [field, out_of((rows, LANES), F32), field, field]
    grads = emitted(ring, width, 2 * units)
    sources = [*weights, *[w for ws in out_weights for w in ws]]
    kernel = functools.partial(
        ffn_first_kernel, len(sources), groups, pairs, len(grads), xs[0].shape[0] // tile
    )
    return call(
        kernel,
        outs + grads,
        [ring.places, *ring.orders, *gs, *xs, *mixed, *sources],
        ins=[SMEM] * groups
        + pair_tiles(gs, tile)
        + pair_tiles(xs, tile)
        + [tiles(a, tile) for a in mixed]
        + [columns(w, 0, w.shape[-1]) for w in sources],
        out_specs=[tiles(o, tile) for o in outs] + [fixed(o) for o in grads],
        grid=(rows // tile,),
        scratch=[
            pltpu.VMEM((width, 2 * units + len(mixed) * LANES), BF),
            pltpu.VMEM((width, 2 * units), F32),
        ],
        mib=56,
        after=after,
    )


def ffn_next_kernel(halves, count, places, unit_ref, scale_ref, *refs):
    g_refs, (out_in, gn_in), refs = refs[:2], refs[2:4], refs[4:]
    sources, refs = refs[:halves], refs[halves:]
    out_ref, mid_ref, act_ref, gpre_ref, w_scr = refs
    units = w_scr.shape[1] // 2

    @pl.when(pl.program_id(0) == 0)
    def _():
        load(places, sources, w_scr, 0)

    win, wout = w_scr[:, :units], w_scr[:, units:]
    unit = unit_ref[...]
    g = pick(count, *g_refs)
    act, slope = gelu_parts(dot(unit, win))
    act = act.astype(BF)
    gpre = (dot(g, wout) * slope).astype(BF)
    act_ref[...] = act
    gpre_ref[...] = gpre
    out_ref[...] = (out_in[...] + dot_cols(act, wout)).astype(BF)
    lead = places[places.shape[0] - 1].astype(F32)
    back = norm_back(gn_in[...] + dot_cols(gpre, win), unit.astype(F32), scale_ref[:, :1])
    mid_ref[...] = (back + lead * g.astype(F32)).astype(BF)


def ffn_next(ring, unit, scale, gs, out, gn, weights, units, tile=512, after=()):
    rows, width = unit.shape
    outs = [out_of((rows, width), BF)] * 2 + [out_of((rows, units), BF)] * 2
    return call(
        functools.partial(ffn_next_kernel, len(weights), gs[0].shape[0] // tile),
        outs,
        [ring.places, unit, scale, *gs, out, gn, *weights],
        ins=[SMEM, tiles(unit, tile), tiles(scale, tile)]
        + pair_tiles(gs, tile)
        + [tiles(out, tile), tiles(gn, tile)]
        + [columns(w, 0, w.shape[-1]) for w in weights],
        out_specs=[tiles(o, tile) for o in outs],
        grid=(rows // tile,),
        scratch=[pltpu.VMEM((width, 2 * units), BF)],
        mib=56,
        after=after,
    )


def ffn_grads_kernel(emits, count, places, unit_ref, *refs):
    g_refs, (gpre_ref, act_ref) = refs[:2], refs[2:4]
    grads, total = refs[4:-1], refs[-1]
    step = pl.program_id(0)
    units = act_ref.shape[1]

    @pl.when(step == 0)
    def _():
        total[...] = jnp.zeros_like(total)

    total[:, :units] += dot_rows(unit_ref[...], gpre_ref[...])
    total[:, units:] += dot_rows(pick(count, *g_refs), act_ref[...])

    @pl.when(step == pl.num_programs(0) - 1)
    def _():
        if emits == 2:
            emit(places, total, *grads)
        else:
            grads[0][...] = total[...]


def ffn_grads(ring, unit, gs, gpre, act, tile=512, after=()):
    rows, width = unit.shape
    cols = 2 * act.shape[1]
    outs = emitted(ring, width, cols)
    return call(
        functools.partial(ffn_grads_kernel, len(outs), gs[0].shape[0] // tile),
        outs,
        [ring.places, unit, *gs, gpre, act],
        ins=[SMEM, tiles(unit, tile)]
        + pair_tiles(gs, tile)
        + [tiles(gpre, tile), tiles(act, tile)],
        out_specs=[fixed(o) for o in outs],
        grid=(rows // tile,),
        scratch=[pltpu.VMEM((width, cols), F32)],
        mib=32,
        after=after,
    )


def middle_kernel(halves, groups, pairs, places, *refs):
    mid_refs, refs = refs[:groups], refs[groups:]
    o_refs, refs = refs[:pairs], refs[pairs:]
    sources, (go_ref, total_ref, w_scr) = refs[:halves], refs[halves:]
    step = pl.program_id(0)

    @pl.when(step == 0)
    def _():
        total_ref[...] = jnp.zeros_like(total_ref)
        load(places, sources, w_scr, 0)

    grad = sum_of(mid_refs).astype(BF)
    go_ref[...] = dot(grad, w_scr[...]).astype(BF)
    total_ref[...] += dot_rows(grad, jnp.concatenate([r[...] for r in o_refs], 1))


def middle_back(ring, mids, mixed, weights, tile=512, after=()):
    rows, width = mids[0].shape
    pairs = len(mixed)
    cols = pairs * LANES
    go, total = out_of((rows, cols), BF), out_of((width, cols), F32)
    return call(
        functools.partial(middle_kernel, len(weights), len(mids), pairs),
        [go, total],
        [ring.places, *mids, *mixed, *weights],
        ins=[SMEM]
        + [tiles(a, tile) for a in (*mids, *mixed)]
        + [columns(w, 0, cols) for w in weights],
        out_specs=[tiles(go, tile), fixed(total)],
        grid=(rows // tile,),
        scratch=[pltpu.VMEM((width, cols), BF)],
        mib=24,
        after=after,
    )


def input_back_kernel(halves, groups, pairs, count, places, short_ref, long_ref, *refs):
    mid_refs, refs = refs[:groups], refs[groups:]
    g_refs, refs = refs[:pairs], refs[pairs:]
    sources, (part_ref, w_scr) = refs[:-2], refs[-2:]

    @pl.when(pl.program_id(0) == 0)
    def _():
        at = 0
        for i in range(0, len(sources), halves):
            at = load(places, sources[i : i + halves], w_scr, at)

    part = dot_cols(jnp.concatenate([r[...] for r in g_refs], 1), w_scr[...])
    scale, unit = rms_parts(pick(count, short_ref, long_ref).astype(F32))
    lead = places[places.shape[0] - 1].astype(F32)
    part_ref[...] = (norm_back(part, unit, scale) + lead * sum_of(mid_refs)).astype(BF)


def input_back(ring, xs, mids, grads, weights, tile=512, after=()):
    rows, width = grads[0].shape[0], xs[0].shape[1]
    pairs = len(grads)
    out = out_of((rows, width), BF)
    return call(
        functools.partial(
            input_back_kernel, len(weights[0][0]), len(mids), pairs, xs[0].shape[0] // tile
        ),
        [out],
        [ring.places, *xs, *mids, *grads, *[a for blocks, _ in weights for a in blocks]],
        ins=[SMEM]
        + pair_tiles(xs, tile)
        + [tiles(a, tile) for a in (*mids, *grads)]
        + [columns(a, 0, count) for blocks, count in weights for a in blocks],
        out_specs=[tiles(out, tile)],
        grid=(rows // tile,),
        scratch=[pltpu.VMEM((width, 3 * pairs * LANES), BF)],
        mib=20,
        after=after,
    )[0]


def pad_cols(array, cols):
    return jnp.pad(array, ((0, 0), (0, cols - array.shape[1]))) if cols > array.shape[1] else array


def on_device(
    sizes,
    x_short,
    x_long,
    len_short,
    len_long,
    boundaries,
    q_weight,
    k_weight,
    v_weight,
    out_weight,
    in_weight,
    ff_out_weight,
    attn_gain,
    ffn_gain,
    bias_table,
    cot_short,
    cot_long,
):
    ring = Ring(sizes)
    quarter = ring.quarter
    width = x_short.shape[2]
    buckets, heads = bias_table.shape
    real = heads * DH
    cols = -(-real // LANES) * LANES
    pairs = cols // LANES
    units = in_weight.shape[1] // 2
    batches = [x.shape[:2] for x in (x_short, x_long)]
    lens = (len_short, len_long)

    xs = [x.reshape(-1, width) for x in (x_short, x_long)]
    gs = [g.reshape(-1, width) for g in (cot_short, cot_long)]

    col_a, col_f = (v.astype(F32)[:, None] for v in (attn_gain, ffn_gain))
    padded = [pad_cols(w, cols) for w in (q_weight, k_weight, v_weight, out_weight)]
    scaled = [(w.astype(F32) * col_a).astype(BF) for w in padded[:3]]
    pieces = [[w[:, p * LANES : (p + 1) * LANES] for w in scaled] for p in range(pairs)]
    own = jnp.concatenate([w for piece in pieces for w in piece] + [padded[3]], 1)[None]
    win = (in_weight.astype(F32) * col_f).astype(BF)
    own1, own2 = (
        jnp.concatenate([w[:, at : at + units] for w in (win, ff_out_weight)], 1)[None]
        for at in (0, units)
    )
    step = 3 * LANES
    z = tuple(range(quarter))
    table = jnp.pad(bias_table.T, ((0, 8 - heads), (0, 0)))

    two = (0, 1)
    wide = own.shape[2]
    got = ring.far(own)
    span = 2 * max(length for _, length in batches)
    near, far = bias_bases(boundaries, table, cols // DH, span, after=[own])
    held, own1 = join([own, *got], [(z, 0, wide)], after=[near], through=[own1])
    got = ring.first(held)
    got1 = ring.far(own1)
    unit = norm(xs, after=[held])
    plan = [(two, 0, step), (two, step, wide)]
    *helds, own2 = join([held, got], plan, after=[unit], through=[own2])
    qkv, more = [blocks_of(ring, h, ring.last(h)) for h in helds]
    out_at = (pairs - 1) * step
    out_w = [m[..., out_at:] for m in more]
    qkvs = [(qkv, 0)] + [(more, p * step) for p in range(pairs - 1)]
    out_ws = [out_w] + list(zip(*[ring.exchange(w) for w in out_w]))

    fwd = []
    after = helds
    for p in range(pairs):
        fwd.append(
            attend(ring, batches, lens, near, unit, *qkvs[p], p, after=after)
        )
        if p == 0:
            held1, own2 = join(
                [own1, *got1], [(z, 0, 2 * units)], after=[fwd[0][0]], through=[own2]
            )
            got1 = ring.first(held1)
            got2 = ring.far(own2)
            after = [held1]
        if p == min(1, pairs - 1):
            z2 = tuple(2 + i for i in z)
            plan = [(two, 0, 2 * units), (z2, 0, 2 * units)]
            held1, held2 = join([held1, got1, own2, *got2], plan, after=[fwd[p][0]])
            got1, got2 = ring.last(held1), ring.first(held2)
            after = [held2]
    mixed = [f[3] for f in fwd]
    others = list(zip(*[ring.exchange(o) for o in mixed]))
    (held2,) = join([held2, got2], [(two, 0, 2 * units)], after=[fwd[-1][0]])
    got2 = ring.last(held2)
    first = blocks_of(ring, held1, got1)
    second = blocks_of(ring, held2, got2)

    unit_f, scale, out, gn, *grad1 = ffn_first(
        ring, gs, xs, [*mixed, *[o for g in others for o in g]], first, out_ws, units, after=[held2]
    )
    keep1, send = halves(ring, grad1)
    got1 = ring.last(send)
    out, mid, act, gpre = ffn_next(ring, unit_f, scale, gs, out, gn, second, units)
    keep1, send, mid, out = fold((keep1, got1, 0), through=[mid, out])
    mids = [mid] + ring.exchange(mid)
    outs = [out] + ring.exchange(out)
    got1 = ring.first(send)
    keep2, send2 = halves(ring, ffn_grads(ring, unit_f, gs, gpre, act, after=[keep1]))
    keep1, *sends, send2 = fold((keep1, got1, 1), after=[keep2], through=[send2])
    got1 = ring.far_all(sends)
    got2 = ring.last(send2)
    go, grad_o = middle_back(ring, mids, mixed, out_w, after=[keep1])

    grads = []
    totals = []
    sums = jnp.zeros((8, LANES), F32)
    after = [keep1]
    for p in range(pairs):
        last = p == pairs - 1
        before, rest = ((), ()) if last else (totals, [grad_o] if p == pairs - 2 else None)
        g, sums, made = attend_back(
            ring,
            batches,
            lens,
            boundaries,
            buckets,
            far,
            unit,
            go,
            fwd[p],
            p,
            sums,
            before,
            rest,
            last,
            after=after,
        )
        grads.append(g)
        if p < pairs - 2:
            totals.append(made[0])
        if p == 0:
            keep2, send2 = fold((keep2, got2, 0), after=[g])
            got2 = ring.first(send2)
            after = [keep2]
        if p == pairs - 2:
            early, send = made
            keep2, *sends, send = fold((keep2, got2, 1), after=[g, *got1], through=[send])
            got2 = ring.far_all(sends)
            got = ring.last(send)
            after = [keep2]
    keep, send = made
    early, early_send, send = fold((early, got, 0), after=got2, through=[send])
    early_got = ring.first(early_send)
    got = ring.last(send)
    weights = [(qkv, step), (more, (pairs - 1) * step)]
    part = input_back(ring, xs, mids, grads, weights, after=[early])
    rows = [slice(0, xs[0].shape[0]), slice(xs[0].shape[0], None)]

    def sums_of(fields):
        return [sum(f[r].astype(F32) for f in fields).astype(BF) for r in rows]

    early, *made = fold(
        (early, early_got, 1), (keep, got, 0), through=[part]
    )
    sends, (keep, send, part) = made[: quarter - 1], made[quarter - 1 :]
    early = [early, *ring.far_all(sends)]
    got = ring.first(send)
    parts = [part] + ring.exchange(part)
    ys = sums_of(outs)
    keep, *sends, part = fold((keep, got, 1), after=ys, through=[parts[0]])
    late = [keep, *ring.far_all(sends)]
    grad_xs = sums_of([part] + parts[1:])
    plan = [
        [(0, 0, units), (1, 0, units)],
        [(0, units, 2 * units), (1, units, 2 * units)],
    ]
    grad_in, grad_ff, gain_f = final(
        [[keep1, *got1], [keep2, *got2]], plan, [0], col_f, [in_weight], after=grad_xs
    )
    plan = [
        [(0, p * step + i * LANES, p * step + (i + 1) * LANES) for p in range(pairs - 1)]
        + [(1, i * LANES, (i + 1) * LANES)]
        for i in range(3)
    ]
    plan += [[(0, (pairs - 1) * step, (pairs - 1) * step + cols)], [(1, step, step + LANES)]]
    gq, gk, gv, grad_o, sums, gain = final(
        [early, late], plan, [0, 1, 2], col_a, padded[:3], carry=[gain_f]
    )
    for other in ring.exchange(gain):
        gain = gain + other
    return (
        ys[0].reshape(x_short.shape),
        ys[1].reshape(x_long.shape),
        grad_xs[0].reshape(x_short.shape),
        grad_xs[1].reshape(x_long.shape),
        gq[:, :real],
        gk[:, :real],
        gv[:, :real],
        grad_o[:, :real],
        grad_in,
        grad_ff,
        gain[:, 0],
        gain[:, 1],
        sums[:heads, :buckets].T,
    )


def solution(mesh):
    sizes = (mesh.shape["dp"], mesh.shape["mp"])
    return jax.shard_map(
        functools.partial(on_device, sizes),
        mesh=mesh,
        in_specs=(
            P("dp", None, None),
            P("dp", None, None),
            P("dp"),
            P("dp"),
            P(),
            P("dp", "mp"),
            P("dp", "mp"),
            P("dp", "mp"),
            P("dp", "mp"),
            P("dp", "mp"),
            P("dp", "mp"),
            P("dp"),
            P("dp"),
            P(None, "mp"),
            P("dp", None, None),
            P("dp", None, None),
        ),
        out_specs=(
            P("dp", None, None),
            P("dp", None, None),
            P("dp", None, None),
            P("dp", None, None),
            P("dp", "mp"),
            P("dp", "mp"),
            P("dp", "mp"),
            P("dp", "mp"),
            P("dp", "mp"),
            P("dp", "mp"),
            P("dp"),
            P("dp"),
            P(None, "mp"),
        ),
        check_vma=False,
    )
```

profile of v0, /device:TPU:0, one launch (start us, length us, event | category | flops | bytes accessed | tf_op | source)
XLA Modules:
  0.0 242.3 jit_solution(8882890096811391677)
XLA Ops:
  3.1 3.0 %collective-permute-start = (bf16[1,48,1536]{2,1,0:T(8,128)(2,1)S(1)}, bf16[1,48,1536]{2,1,0:T(8,128)(2,1)S(1)}, u32[]{:S(2)}, u32[]{:S(2)}) collective-permute-start(bf16[1,48,1536]{2,1,0:T(8,128)(2,1)S(1)} %bitcast.37), channel_id=1, source_target_pairs={{0,8},{2,10},{4,12},{6,14},{8,0},{10,2},{12,4},{14,6},{16,24},{18,... | collective-permute-start | bytes 442376 | tf_op jit(solution)/shard_map/ppermute | solution.py:108
  6.1 2.6 %collective-permute-start.1 = (bf16[1,48,1536]{2,1,0:T(8,128)(2,1)S(1)}, bf16[1,48,1536]{2,1,0:T(8,128)(2,1)S(1)}, u32[]{:S(2)}, u32[]{:S(2)}) collective-permute-start(bf16[1,48,1536]{2,1,0:T(8,128)(2,1)S(1)} %bitcast.38), channel_id=1, source_target_pairs={{0,16},{2,18},{4,20},{6,22},{8,24},{10,26},{12,28},{14,30},{16,0},... | collective-permute-start | bytes 442376 | tf_op jit(solution)/shard_map/ppermute | solution.py:108
  10.7 5.9 %shard_map.255 = (f32[6,128,1024]{2,1,0:T(8,128)S(1)}, f32[6,128,1024]{2,1,0:T(8,128)S(1)}) custom-call(s32[15]{0:T(128)S(1)} %copy-done.78, bf16[8,32]{1,0:T(8,128)(2,1)S(1)} %pad.4.refs_1_, bf16[1,48,1536]{2,1,0:T(8,128)(2,1)S(1)} %bitcast.40), custom_call_target="tpu_custom_call" | custom-call | flops 1000000 | bytes 1000 | tf_op jit(solution)/shard_map/pallas_call | solution.py:70
  24.4 6.7 %collective-permute-done.3.refs_1_ = bf16[4,48,1536]{2,1,0:T(8,128)(2,1)S(1)} collective-permute-done((bf16[4,48,1536]{2,1,0:T(8,128)(2,1)S(1)}, bf16[4,48,1536]{2,1,0:T(8,128)(2,1)S(1)}, u32[]{:S(2)}, u32[]{:S(2)}) %collective-permute-start.3) | collective-permute-done | bytes 589856 | tf_op jit(solution)/shard_map/ppermute | solution.py:124
  36.8 2.4 %collective-permute-start.7 = (bf16[1,48,1536]{2,1,0:T(8,128)(2,1)}, bf16[1,48,1536]{2,1,0:T(8,128)(2,1)}, u32[]{:S(2)}, u32[]{:S(2)}) collective-permute-start(bf16[1,48,1536]{2,1,0:T(8,128)(2,1)} %copy-done.36), channel_id=1, source_target_pairs={{0,16},{2,18},{4,20},{6,22},{8,24},{10,26},{12,28},{14,30},{16,0},... | collective-permute-start | bytes 442376 | tf_op jit(solution)/shard_map/ppermute | solution.py:108
  41.5 7.2 %shard_map.259 = (bf16[2048,256]{1,0:T(8,128)(2,1)S(1)}, bf16[2048,128]{1,0:T(8,128)(2,1)S(1)}, bf16[2048,128]{1,0:T(8,128)(2,1)S(1)}, bf16[2048,128]{1,0:T(8,128)(2,1)}) custom-call(s32[17]{0:T(128)S(1)} %pad_add_fusion.refs_0_.refs_3_, s32[4]{0:T(128)S(1)} %copy-done.76, s32[2]{0:T(128)S(1)} %copy-done.77, ...), custom_call_target="tpu_custom_call" | custom-call | flops 1000000 | bytes 1000 | tf_op jit(solution)/shard_map/pallas_call | solution.py:70
  55.2 2.5 %collective-permute-start.11 = (bf16[1,48,1536]{2,1,0:T(8,128)(2,1)S(1)}, bf16[1,48,1536]{2,1,0:T(8,128)(2,1)S(1)}, u32[]{:S(2)}, u32[]{:S(2)}) collective-permute-start(bf16[1,48,1536]{2,1,0:T(8,128)(2,1)S(1)} %get-tuple-element.110.refs_2_), channel_id=1, source_target_pairs={{0,16},{2,18},{4,20},{6,22},{8,24},{10,26},{12,28},{14,30},{16,0},... | collective-permute-start | bytes 442376 | tf_op jit(solution)/shard_map/ppermute | solution.py:108
  57.9 7.2 %shard_map.261 = (bf16[2048,256]{1,0:T(8,128)(2,1)S(1)}, bf16[2048,128]{1,0:T(8,128)(2,1)S(1)}, bf16[2048,128]{1,0:T(8,128)(2,1)S(1)}, bf16[2048,128]{1,0:T(8,128)(2,1)}) custom-call(s32[17]{0:T(128)S(1)} %pad_add_fusion.refs_0_.refs_3_, s32[4]{0:T(128)S(1)} %copy-done.76, s32[2]{0:T(128)S(1)} %copy-done.77, ...), custom_call_target="tpu_custom_call" | custom-call | flops 1000000 | bytes 1000 | tf_op jit(solution)/shard_map/pallas_call | solution.py:70
  71.9 7.3 %shard_map.263 = (bf16[2048,256]{1,0:T(8,128)(2,1)S(1)}, bf16[2048,128]{1,0:T(8,128)(2,1)S(1)}, bf16[2048,128]{1,0:T(8,128)(2,1)S(1)}, bf16[2048,128]{1,0:T(8,128)(2,1)}) custom-call(s32[17]{0:T(128)S(1)} %pad_add_fusion.refs_0_.refs_3_, s32[4]{0:T(128)S(1)} %copy-done.76, s32[2]{0:T(128)S(1)} %copy-done.77, ...), custom_call_target="tpu_custom_call" | custom-call | flops 1000000 | bytes 1000 | tf_op jit(solution)/shard_map/pallas_call | solution.py:70
  82.3 2.7 %collective-permute-done.19.refs_1_ = bf16[4,48,1536]{2,1,0:T(8,128)(2,1)S(1)} collective-permute-done((bf16[4,48,1536]{2,1,0:T(8,128)(2,1)S(1)}, bf16[4,48,1536]{2,1,0:T(8,128)(2,1)S(1)}, u32[]{:S(2)}, u32[]{:S(2)}) %collective-permute-start.19) | collective-permute-done | bytes 589856 | tf_op jit(solution)/shard_map/ppermute | solution.py:124
  91.0 27.5 %shard_map.265 = (bf16[2048,768]{1,0:T(8,128)(2,1)}, f32[2048,128]{1,0:T(8,128)}, bf16[2048,768]{1,0:T(8,128)(2,1)}, bf16[2048,768]{1,0:T(8,128)(2,1)}, f32[8,48...) custom-call(s32[17]{0:T(128)} %copy-done.74, s32[16]{0:T(128)} %fusion.3.refs_1_, bf16[1024,768]{1,0:T(8,128)(2,1)} %bitcast.27, ...), custom_call_target="tpu_custom_call" | custom-call | flops 1000000 | bytes 1000 | tf_op jit(solution)/shard_map/pallas_call | solution.py:70
  120.5 17.8 %shard_map.266 = (bf16[2048,768]{1,0:T(8,128)(2,1)}, bf16[2048,768]{1,0:T(8,128)(2,1)}, bf16[2048,768]{1,0:T(8,128)(2,1)}, bf16[2048,768]{1,0:T(8,128)(2,1)}) custom-call(s32[17]{0:T(128)} %copy-done.74, bf16[2048,768]{1,0:T(8,128)(2,1)} %get-tuple-element.118.refs_1_, f32[2048,128]{1,0:T(8,128)} %get-tuple-element.119.refs_2_, bf16[1024,768]{1,0:T(8,128)(2,1)} %bitcast.28, ...), custom_call_target="tpu_custom_call" | custom-call | flops 1000000 | bytes 1000 | tf_op jit(solution)/shard_map/pallas_call | solution.py:70
  144.0 6.9 %shard_map.268 = (f32[8,48,1536]{2,1,0:T(8,128)S(1)}, bf16[8,48,1536]{2,1,0:T(8,128)(2,1)S(1)}) custom-call(s32[17]{0:T(128)S(1)} %copy-done.75, bf16[2048,768]{1,0:T(8,128)(2,1)S(1)} %copy-done.10, bf16[1024,768]{1,0:T(8,128)(2,1)S(1)} %bitcast.29, bf16[1024,768]{1,0:T(8,128)(2,1)S(1)} %bitcast.32, bf16[2048,768]{1,0:T(8,128)(2,1)S(1)} %copy-done.24, ...), custom_call_target="tpu_custom_call" | custom-call | flops 1000000 | bytes 1000 | tf_op jit(solution)/shard_map/pallas_call | solution.py:70
  152.2 6.1 %shard_map.270 = (bf16[2048,384]{1,0:T(8,128)(2,1)S(1)}, f32[768,384]{1,0:T(8,128)S(1)}) custom-call(s32[17]{0:T(128)S(1)} %copy-done.75, bf16[2048,768]{1,0:T(8,128)(2,1)} %get-tuple-element.125.refs_1_.refs_3_, bf16[2048,768]{1,0:T(8,128)(2,1)S(1)} %collective-permute-done.23.refs_2_.refs_4_, bf16[2048,128]{1,0:T(8,128)(2,1)} %get-tuple-element.104.refs_6_.refs_3_.refs_9_, ...), custom_call_target="tpu_custom_call" | custom-call | flops 1000000 | bytes 1000 | tf_op jit(solution)/shard_map/pallas_call | solution.py:70
  158.3 8.6 %shard_map.271 = (bf16[2048,384]{1,0:T(8,128)(2,1)S(1)}, f32[8,128]{1,0:T(8,128)S(1)}, f32[768,384]{1,0:T(8,128)S(1)}) custom-call(s32[4]{0:T(128)S(1)} %copy-done.76, s32[2]{0:T(128)S(1)} %copy-done.77, s32[15]{0:T(128)S(1)} %copy-done.79, s32[17]{0:T(128)S(1)} %copy-done.75, bf16[2048,768]{1,0:T(8,128)(2,1)S(1)} %shard_map.257.refs_2_.refs_3_.refs_4_, ...), custom_call_target="tpu_custom_call" | custom-call | flops 1000000 | bytes 1000 | tf_op jit(solution)/shard_map/pallas_call | solution.py:70
  168.9 2.1 collective-permute-start.27
  173.7 9.1 %shard_map.273 = (bf16[2048,384]{1,0:T(8,128)(2,1)S(1)}, f32[8,128]{1,0:T(8,128)S(1)}, f32[8,48,1152]{2,1,0:T(8,128)S(1)}, bf16[8,48,1152]{2,1,0:T(8,128)(2,1)S(1)}) custom-call(s32[4]{0:T(128)S(1)} %copy-done.76, s32[2]{0:T(128)S(1)} %copy-done.77, s32[15]{0:T(128)S(1)} %copy-done.79, s32[17]{0:T(128)S(1)} %copy-done.75, ...), custom_call_target="tpu_custom_call" | custom-call | flops 1000000 | bytes 1000 | tf_op jit(solution)/shard_map/pallas_call | solution.py:70
  190.7 9.1 %shard_map.275 = (bf16[2048,384]{1,0:T(8,128)(2,1)S(1)}, f32[8,128]{1,0:T(8,128)}, f32[8,48,512]{2,1,0:T(8,128)S(1)}, bf16[8,48,512]{2,1,0:T(8,128)(2,1)S(1)}) custom-call(s32[4]{0:T(128)S(1)} %copy-done.76, s32[2]{0:T(128)S(1)} %copy-done.77, s32[15]{0:T(128)S(1)} %copy-done.79, s32[17]{0:T(128)S(1)} %copy-done.75, ...), custom_call_target="tpu_custom_call" | custom-call | flops 1000000 | bytes 1000 | tf_op jit(solution)/shard_map/pallas_call | solution.py:70
  203.3 8.8 %shard_map.277.refs_4_ = bf16[2048,768]{1,0:T(8,128)(2,1)S(1)} custom-call(s32[17]{0:T(128)S(1)} %copy-done.75, bf16[1024,768]{1,0:T(8,128)(2,1)S(1)} %bitcast.23, bf16[1024,768]{1,0:T(8,128)(2,1)S(1)} %bitcast.26, bf16[2048,768]{1,0:T(8,128)(2,1)} %get-tuple-element.125.refs_1_.refs_3_, bf16[2048,768]{1,0:T(8,128)(2,1)S(1)} %collective-permute-done.23.refs_2_.refs_4_, ...), custom_call_target="tpu_custom_call" | custom-call | flops 1000000 | bytes 1000 | tf_op jit(solution)/shard_map/pallas_call | solution.py:70
  216.7 2.2 collective-permute-start.38
  218.9 3.6 %add_convert_fusion.2 = (bf16[1024,768]{1,0:T(8,128)(2,1)S(1)}, bf16[1024,768]{1,0:T(8,128)(2,1)S(1)}) fusion(bf16[2048,768]{1,0:T(8,128)(2,1)} %collective-permute-done.22, bf16[2048,768]{1,0:T(8,128)(2,1)} %get-tuple-element.124), kind=kLoop, calls=%fused_computation.2 | loop fusion | flops 6291456 | bytes 9437184 | tf_op jit(solution)/shard_map/convert_element_type | solution.py:997
  226.7 2.4 collective-permute-start.42
  230.6 2.7 %add_convert_fusion = (bf16[1024,768]{1,0:T(8,128)(2,1)S(1)}, bf16[1024,768]{1,0:T(8,128)(2,1)S(1)}) fusion(bf16[2048,768]{1,0:T(8,128)(2,1)} %collective-permute-done.37, bf16[2048,768]{1,0:T(8,128)(2,1)S(1)} %get-tuple-element.169), kind=kLoop, calls=%fused_computation | loop fusion | flops 6291456 | bytes 9437184 | tf_op jit(solution)/shard_map/convert_element_type | solution.py:997
  235.8 3.4 %collective-permute-done.42.refs_11_ = bf16[48,512]{1,0:T(8,128)(2,1)S(1)} collective-permute-done((bf16[48,512]{1,0:T(8,128)(2,1)S(1)}, bf16[48,512]{1,0:T(8,128)(2,1)S(1)}, u32[]{:S(2)}, u32[]{:S(2)}) %collective-permute-start.42) | collective-permute-done | bytes 49184 | tf_op jit(solution)/shard_map/ppermute | solution.py:114
  (300 shorter events, 82.7 us)
Async XLA Ops:
  3.1 17.3 %collective-permute-start = (bf16[1,48,1536]{2,1,0:T(8,128)(2,1)S(1)}, bf16[1,48,1536]{2,1,0:T(8,128)(2,1)S(1)}, u32[]{:S(2)}, u32[]{:S(2)}) collective-permute-start(bf16[1,48,1536]{2,1,0:T(8,128)(2,1)S(1)} %bitcast.37), channel_id=1, source_target_pairs={{0,8},{2,10},{4,12},{6,14},{8,0},{10,2},{12,4},{14,6},{16,24},{18,... | collective-permute-start | bytes 442376 | tf_op jit(solution)/shard_map/ppermute | solution.py:108
  6.1 14.3 %collective-permute-start.1 = (bf16[1,48,1536]{2,1,0:T(8,128)(2,1)S(1)}, bf16[1,48,1536]{2,1,0:T(8,128)(2,1)S(1)}, u32[]{:S(2)}, u32[]{:S(2)}) collective-permute-start(bf16[1,48,1536]{2,1,0:T(8,128)(2,1)S(1)} %bitcast.38), channel_id=1, source_target_pairs={{0,16},{2,18},{4,20},{6,22},{8,24},{10,26},{12,28},{14,30},{16,0},... | collective-permute-start | bytes 442376 | tf_op jit(solution)/shard_map/ppermute | solution.py:108
  34.5 23.4 %collective-permute-start.5 = (bf16[8,48,1152]{2,1,0:T(8,128)(2,1)}, bf16[8,48,1152]{2,1,0:T(8,128)(2,1)}, u32[]{:S(2)}, u32[]{:S(2)}) collective-permute-start(bf16[8,48,1152]{2,1,0:T(8,128)(2,1)} %get-tuple-element.103.refs_8_.refs_5_.refs_10_), channel_id=1, source_target_pairs={{0,4},{1,3},{2,6},{3,1},{4,0},{5,7},{6,2},{7,5},{8,12},{9,11},{10,... | collective-permute-start | bytes 2654216 | tf_op jit(solution)/shard_map/ppermute | solution.py:124
  34.8 14.7 %collective-permute-start.6 = (bf16[1,48,1536]{2,1,0:T(8,128)(2,1)}, bf16[1,48,1536]{2,1,0:T(8,128)(2,1)}, u32[]{:S(2)}, u32[]{:S(2)}) collective-permute-start(bf16[1,48,1536]{2,1,0:T(8,128)(2,1)} %copy-done.36), channel_id=1, source_target_pairs={{0,8},{2,10},{4,12},{6,14},{8,0},{10,2},{12,4},{14,6},{16,24},{18,... | collective-permute-start | bytes 442376 | tf_op jit(solution)/shard_map/ppermute | solution.py:108
  36.8 12.8 %collective-permute-start.7 = (bf16[1,48,1536]{2,1,0:T(8,128)(2,1)}, bf16[1,48,1536]{2,1,0:T(8,128)(2,1)}, u32[]{:S(2)}, u32[]{:S(2)}) collective-permute-start(bf16[1,48,1536]{2,1,0:T(8,128)(2,1)} %copy-done.36), channel_id=1, source_target_pairs={{0,16},{2,18},{4,20},{6,22},{8,24},{10,26},{12,28},{14,30},{16,0},... | collective-permute-start | bytes 442376 | tf_op jit(solution)/shard_map/ppermute | solution.py:108
  51.8 14.9 %collective-permute-start.9 = (bf16[4,48,1536]{2,1,0:T(8,128)(2,1)S(1)}, bf16[4,48,1536]{2,1,0:T(8,128)(2,1)S(1)}, u32[]{:S(2)}, u32[]{:S(2)}) collective-permute-start(bf16[4,48,1536]{2,1,0:T(8,128)(2,1)S(1)} %get-tuple-element.108.refs_7_.refs_0_), channel_id=1, source_target_pairs={{0,2},{1,5},{2,0},{3,7},{4,6},{5,1},{6,4},{7,3},{8,10},{9,13},{10,... | collective-permute-start | bytes 1769480 | tf_op jit(solution)/shard_map/ppermute | solution.py:124
  67.8 23.2 %collective-permute-start.16 = (bf16[8,48,1536]{2,1,0:T(8,128)(2,1)}, bf16[8,48,1536]{2,1,0:T(8,128)(2,1)}, u32[]{:S(2)}, u32[]{:S(2)}) collective-permute-start(bf16[8,48,1536]{2,1,0:T(8,128)(2,1)} %get-tuple-element.114.refs_12_), channel_id=1, source_target_pairs={{0,4},{1,3},{2,6},{3,1},{4,0},{5,7},{6,2},{7,5},{8,12},{9,11},{10,... | collective-permute-start | bytes 3538952 | tf_op jit(solution)/shard_map/ppermute | solution.py:124
  68.8 16.3 %collective-permute-start.19 = (bf16[4,48,1536]{2,1,0:T(8,128)(2,1)S(1)}, bf16[4,48,1536]{2,1,0:T(8,128)(2,1)S(1)}, u32[]{:S(2)}, u32[]{:S(2)}) collective-permute-start(bf16[4,48,1536]{2,1,0:T(8,128)(2,1)S(1)} %get-tuple-element.112.refs_7_.refs_0_), channel_id=1, source_target_pairs={{0,2},{1,5},{2,0},{3,7},{4,6},{5,1},{6,4},{7,3},{8,10},{9,13},{10,... | collective-permute-start | bytes 1769480 | tf_op jit(solution)/shard_map/ppermute | solution.py:124
  70.9 18.9 %collective-permute-start.13 = (bf16[2048,128]{1,0:T(8,128)(2,1)}, bf16[2048,128]{1,0:T(8,128)(2,1)}, u32[]{:S(2)}, u32[]{:S(2)}) collective-permute-start(bf16[2048,128]{1,0:T(8,128)(2,1)} %get-tuple-element.104.refs_6_.refs_3_.refs_9_), channel_id=1, source_target_pairs={{0,1},{1,0},{2,3},{3,2},{4,5},{5,4},{6,7},{7,6},{8,9},{9,8},{10,11... | collective-permute-start | bytes 1572872 | tf_op jit(solution)/shard_map/ppermute | solution.py:134
  71.8 19.2 %collective-permute-start.14 = (bf16[2048,128]{1,0:T(8,128)(2,1)}, bf16[2048,128]{1,0:T(8,128)(2,1)}, u32[]{:S(2)}, u32[]{:S(2)}) collective-permute-start(bf16[2048,128]{1,0:T(8,128)(2,1)} %get-tuple-element.109.refs_7_.refs_4_.refs_9_), channel_id=1, source_target_pairs={{0,1},{1,0},{2,3},{3,2},{4,5},{5,4},{6,7},{7,6},{8,9},{9,8},{10,11... | collective-permute-start | bytes 1572872 | tf_op jit(solution)/shard_map/ppermute | solution.py:134
  89.8 29.7 %collective-permute-start.21 = (bf16[8,48,1536]{2,1,0:T(8,128)(2,1)S(1)}, bf16[8,48,1536]{2,1,0:T(8,128)(2,1)S(1)}, u32[]{:S(2)}, u32[]{:S(2)}) collective-permute-start(bf16[8,48,1536]{2,1,0:T(8,128)(2,1)S(1)} %shard_map.264.refs_18_.refs_7_), channel_id=1, source_target_pairs={{0,4},{1,3},{2,6},{3,1},{4,0},{5,7},{6,2},{7,5},{8,12},{9,11},{10,... | collective-permute-start | bytes 3538952 | tf_op jit(solution)/shard_map/ppermute | solution.py:124
  118.5 19.8 %collective-permute-start.20 = (bf16[8,48,1536]{2,1,0:T(8,128)(2,1)}, bf16[8,48,1536]{2,1,0:T(8,128)(2,1)S(1)}, u32[]{:S(2)}, u32[]{:S(2)}) collective-permute-start(bf16[8,48,1536]{2,1,0:T(8,128)(2,1)} %get-tuple-element.117), channel_id=1, source_target_pairs={{0,4},{1,3},{2,6},{3,1},{4,0},{5,7},{6,2},{7,5},{8,12},{9,11},{10,... | collective-permute-start | bytes 3538952 | tf_op jit(solution)/shard_map/ppermute | solution.py:124
  138.6 13.5 %collective-permute-start.23 = (bf16[2048,768]{1,0:T(8,128)(2,1)}, bf16[2048,768]{1,0:T(8,128)(2,1)S(1)}, u32[]{:S(2)}, u32[]{:S(2)}) collective-permute-start(bf16[2048,768]{1,0:T(8,128)(2,1)} %get-tuple-element.125.refs_1_.refs_3_), channel_id=1, source_target_pairs={{0,1},{1,0},{2,3},{3,2},{4,5},{5,4},{6,7},{7,6},{8,9},{9,8},{10,11... | collective-permute-start | bytes 9437192 | tf_op jit(solution)/shard_map/ppermute | solution.py:134
  151.0 16.3 %collective-permute-start.25 = (bf16[8,48,1536]{2,1,0:T(8,128)(2,1)S(1)}, bf16[8,48,1536]{2,1,0:T(8,128)(2,1)S(1)}, u32[]{:S(2)}, u32[]{:S(2)}) collective-permute-start(bf16[8,48,1536]{2,1,0:T(8,128)(2,1)S(1)} %get-tuple-element.142), channel_id=1, source_target_pairs={{0,4},{1,3},{2,6},{3,1},{4,0},{5,7},{6,2},{7,5},{8,12},{9,11},{10,... | collective-permute-start | bytes 3538952 | tf_op jit(solution)/shard_map/ppermute | solution.py:124
  167.4 17.3 %collective-permute-start.26 = (bf16[4,48,1536]{2,1,0:T(8,128)(2,1)S(1)}, bf16[4,48,1536]{2,1,0:T(8,128)(2,1)S(1)}, u32[]{:S(2)}, u32[]{:S(2)}) collective-permute-start(bf16[4,48,1536]{2,1,0:T(8,128)(2,1)S(1)} %get-tuple-element.146), channel_id=1, source_target_pairs={{0,2},{1,5},{2,0},{3,7},{4,6},{5,1},{6,4},{7,3},{8,10},{9,13},{10,... | collective-permute-start | bytes 1769480 | tf_op jit(solution)/shard_map/ppermute | solution.py:124
  168.9 13.9 %collective-permute-start.27 = (bf16[48,1536]{1,0:T(8,128)(2,1)S(1)}, bf16[48,1536]{1,0:T(8,128)(2,1)S(1)}, u32[]{:S(2)}, u32[]{:S(2)}) collective-permute-start(bf16[48,1536]{1,0:T(8,128)(2,1)S(1)} %get-tuple-element.148), channel_id=1, source_target_pairs={{0,8},{2,10},{4,12},{6,14},{8,0},{10,2},{12,4},{14,6},{16,24},{18,... | collective-permute-start | bytes 442376 | tf_op jit(solution)/shard_map/ppermute | solution.py:114
  171.0 13.7 %collective-permute-start.28 = (bf16[48,1536]{1,0:T(8,128)(2,1)S(1)}, bf16[48,1536]{1,0:T(8,128)(2,1)S(1)}, u32[]{:S(2)}, u32[]{:S(2)}) collective-permute-start(bf16[48,1536]{1,0:T(8,128)(2,1)S(1)} %get-tuple-element.149), channel_id=1, source_target_pairs={{0,16},{2,18},{4,20},{6,22},{8,24},{10,26},{12,28},{14,30},{16,0},... | collective-permute-start | bytes 442376 | tf_op jit(solution)/shard_map/ppermute | solution.py:114
  172.2 12.5 %collective-permute-start.29 = (bf16[48,1536]{1,0:T(8,128)(2,1)S(1)}, bf16[48,1536]{1,0:T(8,128)(2,1)S(1)}, u32[]{:S(2)}, u32[]{:S(2)}) collective-permute-start(bf16[48,1536]{1,0:T(8,128)(2,1)S(1)} %get-tuple-element.150), channel_id=1, source_target_pairs={{0,24},{2,26},{4,28},{6,30},{8,16},{10,18},{12,20},{14,22},{16,8},... | collective-permute-start | bytes 442376 | tf_op jit(solution)/shard_map/ppermute | solution.py:114
  185.4 15.9 %collective-permute-start.30 = (bf16[8,48,1152]{2,1,0:T(8,128)(2,1)S(1)}, bf16[8,48,1152]{2,1,0:T(8,128)(2,1)S(1)}, u32[]{:S(2)}, u32[]{:S(2)}) collective-permute-start(bf16[8,48,1152]{2,1,0:T(8,128)(2,1)S(1)} %get-tuple-element.152), channel_id=1, source_target_pairs={{0,4},{1,3},{2,6},{3,1},{4,0},{5,7},{6,2},{7,5},{8,12},{9,11},{10,... | collective-permute-start | bytes 2654216 | tf_op jit(solution)/shard_map/ppermute | solution.py:124
  186.0 13.9 %collective-permute-start.31 = (bf16[48,1536]{1,0:T(8,128)(2,1)S(1)}, bf16[48,1536]{1,0:T(8,128)(2,1)S(1)}, u32[]{:S(2)}, u32[]{:S(2)}) collective-permute-start(bf16[48,1536]{1,0:T(8,128)(2,1)S(1)} %get-tuple-element.153), channel_id=1, source_target_pairs={{0,8},{2,10},{4,12},{6,14},{8,0},{10,2},{12,4},{14,6},{16,24},{18,... | collective-permute-start | bytes 442376 | tf_op jit(solution)/shard_map/ppermute | solution.py:114
  188.0 13.3 %collective-permute-start.32 = (bf16[48,1536]{1,0:T(8,128)(2,1)S(1)}, bf16[48,1536]{1,0:T(8,128)(2,1)S(1)}, u32[]{:S(2)}, u32[]{:S(2)}) collective-permute-start(bf16[48,1536]{1,0:T(8,128)(2,1)S(1)} %get-tuple-element.154), channel_id=1, source_target_pairs={{0,16},{2,18},{4,20},{6,22},{8,24},{10,26},{12,28},{14,30},{16,0},... | collective-permute-start | bytes 442376 | tf_op jit(solution)/shard_map/ppermute | solution.py:114
  203.3 15.6 %collective-permute-start.22 = (bf16[2048,768]{1,0:T(8,128)(2,1)}, bf16[2048,768]{1,0:T(8,128)(2,1)}, u32[]{:S(2)}, u32[]{:S(2)}) collective-permute-start(bf16[2048,768]{1,0:T(8,128)(2,1)} %get-tuple-element.124), channel_id=1, source_target_pairs={{0,1},{1,0},{2,3},{3,2},{4,5},{5,4},{6,7},{7,6},{8,9},{9,8},{10,11... | collective-permute-start | bytes 9437192 | tf_op jit(solution)/shard_map/ppermute | solution.py:134
  222.5 13.3 %collective-permute-start.39 = (bf16[48,1152]{1,0:T(8,128)(2,1)S(1)}, bf16[48,1152]{1,0:T(8,128)(2,1)S(1)}, u32[]{:S(2)}, u32[]{:S(2)}) collective-permute-start(bf16[48,1152]{1,0:T(8,128)(2,1)S(1)} %copy-done.84), channel_id=1, source_target_pairs={{0,16},{2,18},{4,20},{6,22},{8,24},{10,26},{12,28},{14,30},{16,0},... | collective-permute-start | bytes 331784 | tf_op jit(solution)/shard_map/ppermute | solution.py:114
  226.7 12.5 %collective-permute-start.42 = (bf16[48,512]{1,0:T(8,128)(2,1)S(1)}, bf16[48,512]{1,0:T(8,128)(2,1)S(1)}, u32[]{:S(2)}, u32[]{:S(2)}) collective-permute-start(bf16[48,512]{1,0:T(8,128)(2,1)S(1)} %get-tuple-element.177), channel_id=1, source_target_pairs={{0,16},{2,18},{4,20},{6,22},{8,24},{10,26},{12,28},{14,30},{16,0},... | collective-permute-start | bytes 147464 | tf_op jit(solution)/shard_map/ppermute | solution.py:114
  (109 other events, 631.0 us)
where the time goes:
time: 247 us; the launch traced here: 242 us
  Pallas kernels  129 us (52%)
  starting transfers between devices  52.8 us (21%)
  local copies, waits for them, and re-layouts  29.3 us (12%)
  waiting for transfers between devices  18.7 us (8%)
  other arithmetic  10.3 us (4%)
    pallas_call x27, Pallas kernels, call(): pl.pallas_call(body, out_shape=list(outs) + [out_of(t.shape, t.dtype) for...  129 us
    unnamed x185, local copies, waits for them, and re-layouts  23.4 us
    ppermute x12, starting transfers between devices, far_all(): lax.ppermute(a, 'dp', [(i, i ^ 4 * (step + 1)) for i in range(self.dp)])  19.7 us
    ppermute x15, starting transfers between devices, near(): return lax.ppermute(array, ('dp', 'mp'), pairs)  16.5 us
    ppermute x9, starting transfers between devices, far(): lax.ppermute(array, 'dp', [(i, i ^ 4 * step) for i in range(self.dp)])  14.4 us
    ppermute x15, waiting for transfers between devices, near(): return lax.ppermute(array, ('dp', 'mp'), pairs)  10 us
    ppermute x12, waiting for transfers between devices, far_all(): lax.ppermute(a, 'dp', [(i, i ^ 4 * (step + 1)) for i in range(self.dp)])  7.4 us
    convert_element_type x2, other arithmetic, sums_of(): return [sum((f[r].astype(F32) for f in fields)).astype(BF) for r in rows]  6.32 us
  transfers between devices with their start and end apart: 45, of which 10 were waited for; matrix products, arithmetic and copies ran while one was open for 5% of the time, Pallas kernels for 52%

commit v1 on v0

--- a/solution.py
+++ b/solution.py
@@ -14,7 +14,6 @@
 BF = jnp.bfloat16
 F32 = jnp.float32
 ANY = pl.BlockSpec(memory_space=pl.ANY)
-HBM = pl.BlockSpec(memory_space=pltpu.HBM)
 SMEM = pl.BlockSpec(memory_space=pltpu.SMEM)
 VMEM = pl.BlockSpec(memory_space=pltpu.VMEM)
 
@@ -57,27 +56,45 @@
     return jax.ShapeDtypeStruct(tuple(shape), kind)
 
 
-def call(kernel, outs, args, *, ins=None, out_specs=None, grid=None, scratch=(), us=0.001, mib=4, after=(), through=()):
+MARKS = {}
+
+
+def mark_of(array):
+    return MARKS[id(array)][1] if id(array) in MARKS else array
+
+
+def call(kernel, outs, args, *, ins=None, out_specs=None, grid=None, scratch=(), mib=4, after=(), through=()):
     ins = list(ins or [VMEM] * len(args))
     out_specs = list(out_specs or [VMEM] * len(outs))
     extra = {} if grid is None else {"grid": grid}
+    after = list({id(m): m for m in map(mark_of, after)}.values())
     idle = len(after) + len(through)
+    mark = out_of((8, LANES), F32)
 
     def body(*refs):
         given, made = refs[: len(args)], refs[len(args) + idle :]
-        kernel(*given, *made[: len(outs)], *made[len(outs) + len(through) :])
-
-    return pl.pallas_call(
+        made[len(outs)][...] = jnp.zeros((8, LANES), F32)
+        kernel(*given, *made[: len(outs)], *made[len(outs) + 1 + len(through) :])
+
+    made = list(
+        pl.pallas_call(
         body,
-        out_shape=list(outs) + [out_of(t.shape, t.dtype) for t in through],
+        out_shape=list(outs) + [mark] + [out_of(t.shape, t.dtype) for t in through],
         in_specs=ins + [ANY] * idle,
-        out_specs=out_specs + [ANY] * len(through),
+        out_specs=out_specs + [VMEM if grid is None else fixed(mark)] + [ANY] * len(through),
         scratch_shapes=list(scratch),
         compiler_params=pltpu.CompilerParams(vmem_limit_bytes=mib << 20),
-        input_output_aliases={len(args) + len(after) + i: len(outs) + i for i in range(len(through))},
-        cost_estimate=pl.CostEstimate(flops=int(us * 1e9), bytes_accessed=1000, transcendentals=0),
+        input_output_aliases={
+            len(args) + len(after) + i: len(outs) + 1 + i for i in range(len(through))
+        },
+        cost_estimate=pl.CostEstimate(flops=1000, bytes_accessed=1000, transcendentals=0),
         **extra,
     )(*args, *after, *through)
+    )
+    mark = made.pop(len(outs))
+    for array in made:
+        MARKS[id(array)] = (array, mark)
+    return made
 
 
 class Ring:
@@ -311,11 +328,11 @@
                 field = jnp.where((row & k) != 0, pltpu.roll(field, k, 1), field)
             while field.shape[0] < LANES:
                 field = jnp.concatenate([field, pltpu.roll(field, field.shape[0], 1)], 0)
-            to[h] = field
+            to[h] = field.astype(BF)
 
 
 def bias_bases(boundaries, table, heads, width, after=()):
-    shape = out_of((heads, LANES, width), F32)
+    shape = out_of((heads, LANES, width), BF)
     return call(
         bases_kernel, [shape, shape], [boundaries, table], ins=[SMEM, VMEM], mib=16, after=after
     )
@@ -395,7 +412,7 @@
                 near_ref[e, :, start - a * LANES : start - a * LANES + length]
                 for a in range(length // LANES)
             ]
-            scores = dot_cols(q_own, k_own) + jnp.concatenate(bias, 0)
+            scores = dot_cols(q_own, k_own) + jnp.concatenate(bias, 0).astype(F32)
             top = jnp.max(scores, 1, keepdims=True)
             expo = jnp.exp(scores - top)
             sums = dot(expo.astype(BF), v_own)
@@ -460,7 +477,7 @@
                 for a in range(length // LANES)
             ]
             bias = jnp.concatenate([far_ref[e, :, c] for c in cols], 0)
-            probs = jnp.exp(dot_cols(k_own, q_own) + bias)
+            probs = jnp.exp(dot_cols(k_own, q_own) + bias.astype(F32))
             ds = probs * dot_cols(v_own, g_own)
             for a, c in enumerate(cols):
                 gbase_ref[e, :, c] += ds[a * LANES : (a + 1) * LANES]
@@ -570,31 +587,6 @@
     return total
 
 
-def add_kernel(count, addends, *refs):
-    value = sum_of(refs[:addends]).astype(BF)
-
-    @pl.when(pl.program_id(0) < count)
-    def _():
-        refs[-2][...] = value
-
-    @pl.when(pl.program_id(0) >= count)
-    def _():
-        refs[-1][...] = value
-
-
-def add_all(shapes, fields, tile=512, after=()):
-    outs = [out_of(s, BF) for s in shapes]
-    return call(
-        functools.partial(add_kernel, shapes[0][0] // tile, len(fields)),
-        outs,
-        fields,
-        ins=[tiles(f, tile) for f in fields],
-        out_specs=pair_tiles(outs, tile),
-        grid=((shapes[0][0] + shapes[1][0]) // tile,),
-        after=after,
-    )
-
-
 def gelu_parts(x):
     c = 0.7978845608028654
     d = c * 0.044715
@@ -675,7 +667,7 @@
             pltpu.VMEM((width, 2 * units + len(mixed) * LANES), BF),
             pltpu.VMEM((width, 2 * units), F32),
         ],
-        mib=56,
+        mib=46,
         after=after,
     )
 
@@ -718,7 +710,7 @@
         out_specs=[tiles(o, tile) for o in outs],
         grid=(rows // tile,),
         scratch=[pltpu.VMEM((width, 2 * units), BF)],
-        mib=56,
+        mib=40,
         after=after,
     )
 
@@ -861,6 +853,7 @@
     cot_short,
     cot_long,
 ):
+    MARKS.clear()
     ring = Ring(sizes)
     quarter = ring.quarter
     width = x_short.shape[2]
@@ -918,7 +911,7 @@
             )
             got1 = ring.first(held1)
             got2 = ring.far(own2)
-            after = [held1]
+            after = [held1, *out_w]
         if p == min(1, pairs - 1):
             z2 = tuple(2 + i for i in z)
             plan = [(two, 0, 2 * units), (z2, 0, 2 * units)]
@@ -1003,8 +996,8 @@
     early = [early, *ring.far_all(sends)]
     got = ring.first(send)
     parts = [part] + ring.exchange(part)
-    ys = sums_of(outs)
-    keep, *sends, part = fold((keep, got, 1), after=ys, through=[parts[0]])
+    keep, *sends, part, out = fold((keep, got, 1), after=[keep], through=[parts[0], outs[0]])
+    ys = sums_of([out] + outs[1:])
     late = [keep, *ring.far_all(sends)]
     grad_xs = sums_of([part] + parts[1:])
     plan = [
@@ -1012,7 +1005,7 @@
         [(0, units, 2 * units), (1, units, 2 * units)],
     ]
     grad_in, grad_ff, gain_f = final(
-        [[keep1, *got1], [keep2, *got2]], plan, [0], col_f, [in_weight], after=grad_xs
+        [[keep1, *got1], [keep2, *got2]], plan, [0], col_f, [in_weight], after=[*grad_xs, *ys]
     )
     plan = [
         [(0, p * step + i * LANES, p * step + (i + 1) * LANES) for p in range(pairs - 1)]

time: 247 us -> 241 us (0.976)
  waiting for transfers between devices: 18.7 us -> 14.1 us
    ppermute x12, waiting for transfers between devices: 7.4 us -> 2.54 us  [far_all(): lax.ppermute(a, 'dp', [(i, i ^ 4 * (step + 1)) for i in range(self.dp)])]
    unnamed x185 -> x151, local copies, waits for them, and re-layouts: 23.4 us -> 23.3 us
  transfers between devices with their start and end apart: 45 -> 45, of which waited for: 10 -> 7; matrix products, arithmetic and copies ran while one was open for 5% -> 6% of each run, Pallas kernels for 52% -> 53%
where the time goes in v1:
time: 241 us; the launch traced here: 237 us
  Pallas kernels  130 us (54%)
  starting transfers between devices  51 us (21%)
  local copies, waits for them, and re-layouts  29.9 us (12%)
  waiting for transfers between devices  14.1 us (6%)
  other arithmetic  10.6 us (4%)
    pallas_call x27, Pallas kernels, call(): pl.pallas_call(body, out_shape=list(outs) + [mark] + [out_of(t.shape, t.d...  130 us
    unnamed x151, local copies, waits for them, and re-layouts  23.3 us
    ppermute x12, starting transfers between devices, far_all(): lax.ppermute(a, 'dp', [(i, i ^ 4 * (step + 1)) for i in range(self.dp)])  18.4 us
    ppermute x15, starting transfers between devices, near(): return lax.ppermute(array, ('dp', 'mp'), pairs)  15.5 us
    ppermute x9, starting transfers between devices, far(): lax.ppermute(array, 'dp', [(i, i ^ 4 * step) for i in range(self.dp)])  15.2 us
    ppermute x15, waiting for transfers between devices, near(): return lax.ppermute(array, ('dp', 'mp'), pairs)  8.8 us
    convert_element_type x2, other arithmetic, sums_of(): return [sum((f[r].astype(F32) for f in fields)).astype(BF) for r in rows]  6.33 us
  transfers between devices with their start and end apart: 45, of which 7 were waited for; matrix products, arithmetic and copies ran while one was open for 6% of the time, Pallas kernels for 53%

profile of v1, /device:TPU:0, one launch (start us, length us, event | category | flops | bytes accessed | tf_op | source)
XLA Modules:
  0.0 237.4 jit_solution(9439777645057802699)
XLA Ops:
  3.2 3.0 %collective-permute-start = (bf16[1,48,1536]{2,1,0:T(8,128)(2,1)S(1)}, bf16[1,48,1536]{2,1,0:T(8,128)(2,1)S(1)}, u32[]{:S(2)}, u32[]{:S(2)}) collective-permute-start(bf16[1,48,1536]{2,1,0:T(8,128)(2,1)S(1)} %bitcast.37), channel_id=1, source_target_pairs={{0,8},{2,10},{4,12},{6,14},{8,0},{10,2},{12,4},{14,6},{16,24},{18,... | collective-permute-start | bytes 442376 | tf_op jit(solution)/shard_map/ppermute | solution.py:125
  6.3 2.6 %collective-permute-start.1 = (bf16[1,48,1536]{2,1,0:T(8,128)(2,1)S(1)}, bf16[1,48,1536]{2,1,0:T(8,128)(2,1)S(1)}, u32[]{:S(2)}, u32[]{:S(2)}) collective-permute-start(bf16[1,48,1536]{2,1,0:T(8,128)(2,1)S(1)} %bitcast.38), channel_id=1, source_target_pairs={{0,16},{2,18},{4,20},{6,22},{8,24},{10,26},{12,28},{14,30},{16,0},... | collective-permute-start | bytes 442376 | tf_op jit(solution)/shard_map/ppermute | solution.py:125
  10.8 4.0 %shard_map.255 = (bf16[6,128,1024]{2,1,0:T(8,128)(2,1)S(1)}, bf16[6,128,1024]{2,1,0:T(8,128)(2,1)S(1)}, f32[8,128]{1,0:T(8,128)S(1)}) custom-call(s32[15]{0:T(128)S(1)} %copy-done.66, bf16[8,32]{1,0:T(8,128)(2,1)S(1)} %pad.4.refs_1_, bf16[1,48,1536]{2,1,0:T(8,128)(2,1)S(1)} %bitcast.40), custom_call_target="tpu_custom_call" | custom-call | flops 1000 | bytes 1000 | tf_op jit(solution)/shard_map/pallas_call | solution.py:80
  18.1 2.1 collective-permute-done.1.refs_2_
  25.4 4.9 %collective-permute-done.3.refs_1_ = bf16[4,48,1536]{2,1,0:T(8,128)(2,1)S(1)} collective-permute-done((bf16[4,48,1536]{2,1,0:T(8,128)(2,1)S(1)}, bf16[4,48,1536]{2,1,0:T(8,128)(2,1)S(1)}, u32[]{:S(2)}, u32[]{:S(2)}) %collective-permute-start.3) | collective-permute-done | bytes 589856 | tf_op jit(solution)/shard_map/ppermute | solution.py:141
  33.5 2.3 collective-permute-start.6
  39.9 7.2 %shard_map.259 = (bf16[2048,256]{1,0:T(8,128)(2,1)S(1)}, bf16[2048,128]{1,0:T(8,128)(2,1)S(1)}, bf16[2048,128]{1,0:T(8,128)(2,1)S(1)}, bf16[2048,128]{1,0:T(8,128)(2,1)}, f32[8,128]{1,0:T(8,128)S(1)}) custom-call(s32[17]{0:T(128)S(1)} %pad_add_fusion.refs_0_.refs_3_, s32[4]{0:T(128)S(1)} %copy-done.64, s32[2]{0:T(128)S(1)} %copy-done.65, ...), custom_call_target="tpu_custom_call" | custom-call | flops 1000 | bytes 1000 | tf_op jit(solution)/shard_map/pallas_call | solution.py:80
  51.1 2.3 collective-permute-start.10
  58.6 7.2 %shard_map.261 = (bf16[2048,256]{1,0:T(8,128)(2,1)S(1)}, bf16[2048,128]{1,0:T(8,128)(2,1)S(1)}, bf16[2048,128]{1,0:T(8,128)(2,1)S(1)}, bf16[2048,128]{1,0:T(8,128)(2,1)}, f32[8,128]{1,0:T(8,128)S(1)}) custom-call(s32[17]{0:T(128)S(1)} %pad_add_fusion.refs_0_.refs_3_, s32[4]{0:T(128)S(1)} %copy-done.64, s32[2]{0:T(128)S(1)} %copy-done.65, ...), custom_call_target="tpu_custom_call" | custom-call | flops 1000 | bytes 1000 | tf_op jit(solution)/shard_map/pallas_call | solution.py:80
  66.6 2.2 shard_map.262
  71.9 7.2 %shard_map.263 = (bf16[2048,256]{1,0:T(8,128)(2,1)S(1)}, bf16[2048,128]{1,0:T(8,128)(2,1)S(1)}, bf16[2048,128]{1,0:T(8,128)(2,1)S(1)}, bf16[2048,128]{1,0:T(8,128)(2,1)}, f32[8,128]{1,0:T(8,128)S(1)}) custom-call(s32[17]{0:T(128)S(1)} %pad_add_fusion.refs_0_.refs_3_, s32[4]{0:T(128)S(1)} %copy-done.64, s32[2]{0:T(128)S(1)} %copy-done.65, ...), custom_call_target="tpu_custom_call" | custom-call | flops 1000 | bytes 1000 | tf_op jit(solution)/shard_map/pallas_call | solution.py:80
  82.9 3.7 %collective-permute-done.19.refs_1_ = bf16[4,48,1536]{2,1,0:T(8,128)(2,1)S(1)} collective-permute-done((bf16[4,48,1536]{2,1,0:T(8,128)(2,1)S(1)}, bf16[4,48,1536]{2,1,0:T(8,128)(2,1)S(1)}, u32[]{:S(2)}, u32[]{:S(2)}) %collective-permute-start.19) | collective-permute-done | bytes 589856 | tf_op jit(solution)/shard_map/ppermute | solution.py:141
  91.2 26.8 %shard_map.265 = (bf16[2048,768]{1,0:T(8,128)(2,1)}, f32[2048,128]{1,0:T(8,128)S(1)}, bf16[2048,768]{1,0:T(8,128)(2,1)}, bf16[2048,768]{1,0:T(8,128)(2,1)}, f32[...) custom-call(s32[17]{0:T(128)S(1)} %pad_add_fusion.refs_0_.refs_3_, s32[16]{0:T(128)S(1)} %fusion.3.refs_1_, ...), custom_call_target="tpu_custom_call" | custom-call | flops 1000 | bytes 1000 | tf_op jit(solution)/shard_map/pallas_call | solution.py:80
  119.6 15.8 %shard_map.266 = (bf16[2048,768]{1,0:T(8,128)(2,1)}, bf16[2048,768]{1,0:T(8,128)(2,1)S(1)}, bf16[2048,768]{1,0:T(8,128)(2,1)}, bf16[2048,768]{1,0:T(8,128)(2,1)}, f32[8,128]{1,0:T(8,128)}) custom-call(s32[17]{0:T(128)S(1)} %pad_add_fusion.refs_0_.refs_3_, bf16[2048,768]{1,0:T(8,128)(2,1)} %get-tuple-element.149.refs_1_, ...), custom_call_target="tpu_custom_call" | custom-call | flops 1000 | bytes 1000 | tf_op jit(solution)/shard_map/pallas_call | solution.py:80
  140.9 7.0 %shard_map.268 = (f32[8,48,1536]{2,1,0:T(8,128)S(1)}, bf16[8,48,1536]{2,1,0:T(8,128)(2,1)S(1)}, f32[8,128]{1,0:T(8,128)S(1)}) custom-call(s32[17]{0:T(128)S(1)} %pad_add_fusion.refs_0_.refs_3_, bf16[2048,768]{1,0:T(8,128)(2,1)S(1)} %copy-done.10, bf16[1024,768]{1,0:T(8,128)(2,1)S(1)} %bitcast.23, bf16[1024,768]{1,0:T(8,128)(2,1)S(1)} %bitcast.26, ...), custom_call_target="tpu_custom_call" | custom-call | flops 1000 | bytes 1000 | tf_op jit(solution)/shard_map/pallas_call | solution.py:80
  149.3 6.9 %shard_map.270 = (bf16[2048,384]{1,0:T(8,128)(2,1)S(1)}, f32[768,384]{1,0:T(8,128)S(1)}, f32[8,128]{1,0:T(8,128)}) custom-call(s32[17]{0:T(128)S(1)} %pad_add_fusion.refs_0_.refs_3_, bf16[2048,768]{1,0:T(8,128)(2,1)S(1)} %get-tuple-element.156.refs_1_.refs_3_, bf16[2048,768]{1,0:T(8,128)(2,1)S(1)} %collective-permute-done.22.refs_2_.refs_4_, ...), custom_call_target="tpu_custom_call" | custom-call | flops 1000 | bytes 1000 | tf_op jit(solution)/shard_map/pallas_call | solution.py:80
  156.2 8.7 %shard_map.271 = (bf16[2048,384]{1,0:T(8,128)(2,1)S(1)}, f32[8,128]{1,0:T(8,128)S(1)}, f32[768,384]{1,0:T(8,128)S(1)}, f32[8,128]{1,0:T(8,128)S(1)}) custom-call(s32[4]{0:T(128)S(1)} %copy-done.64, s32[2]{0:T(128)S(1)} %copy-done.65, s32[15]{0:T(128)S(1)} %copy-done.67, s32[17]{0:T(128)S(1)} %pad_add_fusion.refs_0_.refs_3_, ...), custom_call_target="tpu_custom_call" | custom-call | flops 1000 | bytes 1000 | tf_op jit(solution)/shard_map/pallas_call | solution.py:80
  170.3 9.2 %shard_map.273 = (bf16[2048,384]{1,0:T(8,128)(2,1)S(1)}, f32[8,128]{1,0:T(8,128)S(1)}, f32[8,48,1152]{2,1,0:T(8,128)S(1)}, bf16[8,48,1152]{2,1,0:T(8,128)(2,1)S(1)}, f32[8,128]{1,0:T(8,128)S(1)}) custom-call(s32[4]{0:T(128)S(1)} %copy-done.64, s32[2]{0:T(128)S(1)} %copy-done.65, s32[15]{0:T(128)S(1)} %copy-done.67, s32[17]{0:T(128)S(1)} %pad_add_fusion.refs_0_.refs_3_, ...), custom_call_target="tpu_custom_call" | custom-call | flops 1000 | bytes 1000 | tf_op jit(solution)/shard_map/pallas_call | solution.py:80
  183.0 2.1 collective-permute-start.30
  187.6 9.4 %shard_map.275 = (bf16[2048,384]{1,0:T(8,128)(2,1)S(1)}, f32[8,128]{1,0:T(8,128)}, f32[8,48,512]{2,1,0:T(8,128)S(1)}, bf16[8,48,512]{2,1,0:T(8,128)(2,1)S(1)}, f32[8,128]{1,0:T(8,128)}) custom-call(s32[4]{0:T(128)S(1)} %copy-done.64, s32[2]{0:T(128)S(1)} %copy-done.65, s32[15]{0:T(128)S(1)} %copy-done.67, s32[17]{0:T(128)S(1)} %pad_add_fusion.refs_0_.refs_3_, ...), custom_call_target="tpu_custom_call" | custom-call | flops 1000 | bytes 1000 | tf_op jit(solution)/shard_map/pallas_call | solution.py:80
  200.6 9.0 %shard_map.277 = (bf16[2048,768]{1,0:T(8,128)(2,1)S(1)}, f32[8,128]{1,0:T(8,128)}) custom-call(s32[17]{0:T(128)S(1)} %pad_add_fusion.refs_0_.refs_3_, bf16[1024,768]{1,0:T(8,128)(2,1)S(1)} %bitcast.29, bf16[1024,768]{1,0:T(8,128)(2,1)S(1)} %bitcast.32, bf16[2048,768]{1,0:T(8,128)(2,1)S(1)} %get-tuple-element.156.refs_1_.refs_3_, ...), custom_call_target="tpu_custom_call" | custom-call | flops 1000 | bytes 1000 | tf_op jit(solution)/shard_map/pallas_call | solution.py:80
  213.9 2.0 collective-permute-start.38
  224.4 3.6 %add_convert_fusion.2 = (bf16[1024,768]{1,0:T(8,128)(2,1)S(1)}, bf16[1024,768]{1,0:T(8,128)(2,1)S(1)}) fusion(bf16[2048,768]{1,0:T(8,128)(2,1)} %collective-permute-done.36, bf16[2048,768]{1,0:T(8,128)(2,1)} %get-tuple-element.212), kind=kLoop, calls=%fused_computation.2 | loop fusion | flops 6291456 | bytes 9437184 | tf_op jit(solution)/shard_map/convert_element_type | solution.py:990
  229.6 2.7 %add_convert_fusion = (bf16[1024,768]{1,0:T(8,128)(2,1)S(1)}, bf16[1024,768]{1,0:T(8,128)(2,1)S(1)}) fusion(bf16[2048,768]{1,0:T(8,128)(2,1)} %collective-permute-done.37, bf16[2048,768]{1,0:T(8,128)(2,1)S(1)} %get-tuple-element.213), kind=kLoop, calls=%fused_computation | loop fusion | flops 6291456 | bytes 9437184 | tf_op jit(solution)/shard_map/convert_element_type | solution.py:990
  (266 shorter events, 83.5 us)
Async XLA Ops:
  3.2 14.9 %collective-permute-start = (bf16[1,48,1536]{2,1,0:T(8,128)(2,1)S(1)}, bf16[1,48,1536]{2,1,0:T(8,128)(2,1)S(1)}, u32[]{:S(2)}, u32[]{:S(2)}) collective-permute-start(bf16[1,48,1536]{2,1,0:T(8,128)(2,1)S(1)} %bitcast.37), channel_id=1, source_target_pairs={{0,8},{2,10},{4,12},{6,14},{8,0},{10,2},{12,4},{14,6},{16,24},{18,... | collective-permute-start | bytes 442376 | tf_op jit(solution)/shard_map/ppermute | solution.py:125
  6.3 14.0 %collective-permute-start.1 = (bf16[1,48,1536]{2,1,0:T(8,128)(2,1)S(1)}, bf16[1,48,1536]{2,1,0:T(8,128)(2,1)S(1)}, u32[]{:S(2)}, u32[]{:S(2)}) collective-permute-start(bf16[1,48,1536]{2,1,0:T(8,128)(2,1)S(1)} %bitcast.38), channel_id=1, source_target_pairs={{0,16},{2,18},{4,20},{6,22},{8,24},{10,26},{12,28},{14,30},{16,0},... | collective-permute-start | bytes 442376 | tf_op jit(solution)/shard_map/ppermute | solution.py:125
  33.0 23.9 %collective-permute-start.5 = (bf16[8,48,1152]{2,1,0:T(8,128)(2,1)}, bf16[8,48,1152]{2,1,0:T(8,128)(2,1)}, u32[]{:S(2)}, u32[]{:S(2)}) collective-permute-start(bf16[8,48,1152]{2,1,0:T(8,128)(2,1)} %get-tuple-element.132.refs_5_.refs_10_), channel_id=1, source_target_pairs={{0,4},{1,3},{2,6},{3,1},{4,0},{5,7},{6,2},{7,5},{8,12},{9,11},{10,... | collective-permute-start | bytes 2654216 | tf_op jit(solution)/shard_map/ppermute | solution.py:141
  33.5 14.7 %collective-permute-start.6 = (bf16[1,48,1536]{2,1,0:T(8,128)(2,1)S(1)}, bf16[1,48,1536]{2,1,0:T(8,128)(2,1)S(1)}, u32[]{:S(2)}, u32[]{:S(2)}) collective-permute-start(bf16[1,48,1536]{2,1,0:T(8,128)(2,1)S(1)} %get-tuple-element.133.refs_0_), channel_id=1, source_target_pairs={{0,8},{2,10},{4,12},{6,14},{8,0},{10,2},{12,4},{14,6},{16,24},{18,... | collective-permute-start | bytes 442376 | tf_op jit(solution)/shard_map/ppermute | solution.py:125
  49.5 17.1 %collective-permute-start.9 = (bf16[4,48,1536]{2,1,0:T(8,128)(2,1)S(1)}, bf16[4,48,1536]{2,1,0:T(8,128)(2,1)S(1)}, u32[]{:S(2)}, u32[]{:S(2)}) collective-permute-start(bf16[4,48,1536]{2,1,0:T(8,128)(2,1)S(1)} %get-tuple-element.138.refs_0_), channel_id=1, source_target_pairs={{0,2},{1,5},{2,0},{3,7},{4,6},{5,1},{6,4},{7,3},{8,10},{9,13},{10,... | collective-permute-start | bytes 1769480 | tf_op jit(solution)/shard_map/ppermute | solution.py:141
  51.1 15.5 %collective-permute-start.10 = (bf16[1,48,1536]{2,1,0:T(8,128)(2,1)}, bf16[1,48,1536]{2,1,0:T(8,128)(2,1)S(1)}, u32[]{:S(2)}, u32[]{:S(2)}) collective-permute-start(bf16[1,48,1536]{2,1,0:T(8,128)(2,1)} %get-tuple-element.139.refs_2_), channel_id=1, source_target_pairs={{0,8},{2,10},{4,12},{6,14},{8,0},{10,2},{12,4},{14,6},{16,24},{18,... | collective-permute-start | bytes 442376 | tf_op jit(solution)/shard_map/ppermute | solution.py:125
  53.4 13.2 %collective-permute-start.11 = (bf16[1,48,1536]{2,1,0:T(8,128)(2,1)}, bf16[1,48,1536]{2,1,0:T(8,128)(2,1)S(1)}, u32[]{:S(2)}, u32[]{:S(2)}) collective-permute-start(bf16[1,48,1536]{2,1,0:T(8,128)(2,1)} %get-tuple-element.139.refs_2_), channel_id=1, source_target_pairs={{0,16},{2,18},{4,20},{6,22},{8,24},{10,26},{12,28},{14,30},{16,0},... | collective-permute-start | bytes 442376 | tf_op jit(solution)/shard_map/ppermute | solution.py:125
  68.8 21.4 %collective-permute-start.16 = (bf16[8,48,1536]{2,1,0:T(8,128)(2,1)}, bf16[8,48,1536]{2,1,0:T(8,128)(2,1)}, u32[]{:S(2)}, u32[]{:S(2)}) collective-permute-start(bf16[8,48,1536]{2,1,0:T(8,128)(2,1)} %get-tuple-element.143.refs_12_), channel_id=1, source_target_pairs={{0,4},{1,3},{2,6},{3,1},{4,0},{5,7},{6,2},{7,5},{8,12},{9,11},{10,... | collective-permute-start | bytes 3538952 | tf_op jit(solution)/shard_map/ppermute | solution.py:141
  70.3 16.3 %collective-permute-start.19 = (bf16[4,48,1536]{2,1,0:T(8,128)(2,1)S(1)}, bf16[4,48,1536]{2,1,0:T(8,128)(2,1)S(1)}, u32[]{:S(2)}, u32[]{:S(2)}) collective-permute-start(bf16[4,48,1536]{2,1,0:T(8,128)(2,1)S(1)} %get-tuple-element.144.refs_0_), channel_id=1, source_target_pairs={{0,2},{1,5},{2,0},{3,7},{4,6},{5,1},{6,4},{7,3},{8,10},{9,13},{10,... | collective-permute-start | bytes 1769480 | tf_op jit(solution)/shard_map/ppermute | solution.py:141
  71.3 18.4 %collective-permute-start.13 = (bf16[2048,128]{1,0:T(8,128)(2,1)}, bf16[2048,128]{1,0:T(8,128)(2,1)}, u32[]{:S(2)}, u32[]{:S(2)}) collective-permute-start(bf16[2048,128]{1,0:T(8,128)(2,1)} %get-tuple-element.131.refs_6_.refs_3_.refs_9_), channel_id=1, source_target_pairs={{0,1},{1,0},{2,3},{3,2},{4,5},{5,4},{6,7},{7,6},{8,9},{9,8},{10,11... | collective-permute-start | bytes 1572872 | tf_op jit(solution)/shard_map/ppermute | solution.py:151
  71.8 18.5 %collective-permute-start.14 = (bf16[2048,128]{1,0:T(8,128)(2,1)}, bf16[2048,128]{1,0:T(8,128)(2,1)}, u32[]{:S(2)}, u32[]{:S(2)}) collective-permute-start(bf16[2048,128]{1,0:T(8,128)(2,1)} %get-tuple-element.137.refs_7_.refs_4_.refs_9_), channel_id=1, source_target_pairs={{0,1},{1,0},{2,3},{3,2},{4,5},{5,4},{6,7},{7,6},{8,9},{9,8},{10,11... | collective-permute-start | bytes 1572872 | tf_op jit(solution)/shard_map/ppermute | solution.py:151
  89.6 30.0 %collective-permute-start.21 = (bf16[8,48,1536]{2,1,0:T(8,128)(2,1)S(1)}, bf16[8,48,1536]{2,1,0:T(8,128)(2,1)S(1)}, u32[]{:S(2)}, u32[]{:S(2)}) collective-permute-start(bf16[8,48,1536]{2,1,0:T(8,128)(2,1)S(1)} %get-tuple-element.153.refs_7_), channel_id=1, source_target_pairs={{0,4},{1,3},{2,6},{3,1},{4,0},{5,7},{6,2},{7,5},{8,12},{9,11},{10,... | collective-permute-start | bytes 3538952 | tf_op jit(solution)/shard_map/ppermute | solution.py:141
  118.1 17.4 %collective-permute-start.20 = (bf16[8,48,1536]{2,1,0:T(8,128)(2,1)S(1)}, bf16[8,48,1536]{2,1,0:T(8,128)(2,1)S(1)}, u32[]{:S(2)}, u32[]{:S(2)}) collective-permute-start(bf16[8,48,1536]{2,1,0:T(8,128)(2,1)S(1)} %get-tuple-element.148), channel_id=1, source_target_pairs={{0,4},{1,3},{2,6},{3,1},{4,0},{5,7},{6,2},{7,5},{8,12},{9,11},{10,... | collective-permute-start | bytes 3538952 | tf_op jit(solution)/shard_map/ppermute | solution.py:141
  148.7 16.3 %collective-permute-start.24 = (bf16[8,48,1536]{2,1,0:T(8,128)(2,1)S(1)}, bf16[8,48,1536]{2,1,0:T(8,128)(2,1)S(1)}, u32[]{:S(2)}, u32[]{:S(2)}) collective-permute-start(bf16[8,48,1536]{2,1,0:T(8,128)(2,1)S(1)} %get-tuple-element.177), channel_id=1, source_target_pairs={{0,4},{1,3},{2,6},{3,1},{4,0},{5,7},{6,2},{7,5},{8,12},{9,11},{10,... | collective-permute-start | bytes 3538952 | tf_op jit(solution)/shard_map/ppermute | solution.py:141
  165.3 16.2 %collective-permute-start.25 = (bf16[4,48,1536]{2,1,0:T(8,128)(2,1)S(1)}, bf16[4,48,1536]{2,1,0:T(8,128)(2,1)S(1)}, u32[]{:S(2)}, u32[]{:S(2)}) collective-permute-start(bf16[4,48,1536]{2,1,0:T(8,128)(2,1)S(1)} %get-tuple-element.182), channel_id=1, source_target_pairs={{0,2},{1,5},{2,0},{3,7},{4,6},{5,1},{6,4},{7,3},{8,10},{9,13},{10,... | collective-permute-start | bytes 1769480 | tf_op jit(solution)/shard_map/ppermute | solution.py:141
  165.9 13.6 %collective-permute-start.26 = (bf16[48,1536]{1,0:T(8,128)(2,1)S(1)}, bf16[48,1536]{1,0:T(8,128)(2,1)S(1)}, u32[]{:S(2)}, u32[]{:S(2)}) collective-permute-start(bf16[48,1536]{1,0:T(8,128)(2,1)S(1)} %get-tuple-element.184), channel_id=1, source_target_pairs={{0,8},{2,10},{4,12},{6,14},{8,0},{10,2},{12,4},{14,6},{16,24},{18,... | collective-permute-start | bytes 442376 | tf_op jit(solution)/shard_map/ppermute | solution.py:131
  167.7 13.7 %collective-permute-start.27 = (bf16[48,1536]{1,0:T(8,128)(2,1)S(1)}, bf16[48,1536]{1,0:T(8,128)(2,1)S(1)}, u32[]{:S(2)}, u32[]{:S(2)}) collective-permute-start(bf16[48,1536]{1,0:T(8,128)(2,1)S(1)} %get-tuple-element.185), channel_id=1, source_target_pairs={{0,16},{2,18},{4,20},{6,22},{8,24},{10,26},{12,28},{14,30},{16,0},... | collective-permute-start | bytes 442376 | tf_op jit(solution)/shard_map/ppermute | solution.py:131
  182.3 15.3 %collective-permute-start.29 = (bf16[8,48,1152]{2,1,0:T(8,128)(2,1)S(1)}, bf16[8,48,1152]{2,1,0:T(8,128)(2,1)S(1)}, u32[]{:S(2)}, u32[]{:S(2)}) collective-permute-start(bf16[8,48,1152]{2,1,0:T(8,128)(2,1)S(1)} %get-tuple-element.188), channel_id=1, source_target_pairs={{0,4},{1,3},{2,6},{3,1},{4,0},{5,7},{6,2},{7,5},{8,12},{9,11},{10,... | collective-permute-start | bytes 2654216 | tf_op jit(solution)/shard_map/ppermute | solution.py:141
  183.0 14.0 %collective-permute-start.30 = (bf16[48,1536]{1,0:T(8,128)(2,1)S(1)}, bf16[48,1536]{1,0:T(8,128)(2,1)S(1)}, u32[]{:S(2)}, u32[]{:S(2)}) collective-permute-start(bf16[48,1536]{1,0:T(8,128)(2,1)S(1)} %get-tuple-element.189), channel_id=1, source_target_pairs={{0,8},{2,10},{4,12},{6,14},{8,0},{10,2},{12,4},{14,6},{16,24},{18,... | collective-permute-start | bytes 442376 | tf_op jit(solution)/shard_map/ppermute | solution.py:131
  200.6 16.5 %collective-permute-start.36 = (bf16[2048,768]{1,0:T(8,128)(2,1)}, bf16[2048,768]{1,0:T(8,128)(2,1)}, u32[]{:S(2)}, u32[]{:S(2)}) collective-permute-start(bf16[2048,768]{1,0:T(8,128)(2,1)} %get-tuple-element.211.refs_4_), channel_id=1, source_target_pairs={{0,1},{1,0},{2,3},{3,2},{4,5},{5,4},{6,7},{7,6},{8,9},{9,8},{10,11... | collective-permute-start | bytes 9437192 | tf_op jit(solution)/shard_map/ppermute | solution.py:151
  213.9 14.1 %collective-permute-start.38 = (bf16[48,1152]{1,0:T(8,128)(2,1)}, bf16[48,1152]{1,0:T(8,128)(2,1)S(1)}, u32[]{:S(2)}, u32[]{:S(2)}) collective-permute-start(bf16[48,1152]{1,0:T(8,128)(2,1)} %copy-done.70), channel_id=1, source_target_pairs={{0,8},{2,10},{4,12},{6,14},{8,0},{10,2},{12,4},{14,6},{16,24},{18,... | collective-permute-start | bytes 331784 | tf_op jit(solution)/shard_map/ppermute | solution.py:131
  216.0 18.2 %collective-permute-start.39 = (bf16[48,1152]{1,0:T(8,128)(2,1)}, bf16[48,1152]{1,0:T(8,128)(2,1)S(1)}, u32[]{:S(2)}, u32[]{:S(2)}) collective-permute-start(bf16[48,1152]{1,0:T(8,128)(2,1)} %copy-done.69), channel_id=1, source_target_pairs={{0,16},{2,18},{4,20},{6,22},{8,24},{10,26},{12,28},{14,30},{16,0},... | collective-permute-start | bytes 331784 | tf_op jit(solution)/shard_map/ppermute | solution.py:131
  217.1 17.2 %collective-permute-start.40 = (bf16[48,1152]{1,0:T(8,128)(2,1)}, bf16[48,1152]{1,0:T(8,128)(2,1)S(1)}, u32[]{:S(2)}, u32[]{:S(2)}) collective-permute-start(bf16[48,1152]{1,0:T(8,128)(2,1)} %copy-done.68), channel_id=1, source_target_pairs={{0,24},{2,26},{4,28},{6,30},{8,16},{10,18},{12,20},{14,22},{16,8},... | collective-permute-start | bytes 331784 | tf_op jit(solution)/shard_map/ppermute | solution.py:131
  221.0 13.2 %collective-permute-start.41 = (bf16[48,512]{1,0:T(8,128)(2,1)S(1)}, bf16[48,512]{1,0:T(8,128)(2,1)S(1)}, u32[]{:S(2)}, u32[]{:S(2)}) collective-permute-start(bf16[48,512]{1,0:T(8,128)(2,1)S(1)} %get-tuple-element.222), channel_id=1, source_target_pairs={{0,8},{2,10},{4,12},{6,14},{8,0},{10,2},{12,4},{14,6},{16,24},{18,... | collective-permute-start | bytes 147464 | tf_op jit(solution)/shard_map/ppermute | solution.py:131
  (92 other events, 547.3 us)

commit v2 on v1

--- a/solution.py
+++ b/solution.py
@@ -12,6 +12,8 @@
 EPS = 1e-06
 NEG = -1000000000.0
 BF = jnp.bfloat16
+C1 = 1.5
+C2 = 6.0
 F32 = jnp.float32
 ANY = pl.BlockSpec(memory_space=pl.ANY)
 SMEM = pl.BlockSpec(memory_space=pltpu.SMEM)
@@ -63,7 +65,7 @@
     return MARKS[id(array)][1] if id(array) in MARKS else array
 
 
-def call(kernel, outs, args, *, ins=None, out_specs=None, grid=None, scratch=(), mib=4, after=(), through=()):
+def call(kernel, outs, args, *, ins=None, out_specs=None, grid=None, scratch=(), us=0.001, mib=4, after=(), through=()):
     ins = list(ins or [VMEM] * len(args))
     out_specs = list(out_specs or [VMEM] * len(outs))
     extra = {} if grid is None else {"grid": grid}
@@ -87,7 +89,7 @@
         input_output_aliases={
             len(args) + len(after) + i: len(outs) + 1 + i for i in range(len(through))
         },
-        cost_estimate=pl.CostEstimate(flops=1000, bytes_accessed=1000, transcendentals=0),
+        cost_estimate=pl.CostEstimate(flops=int(us * 1e9), bytes_accessed=1000, transcendentals=0),
         **extra,
     )(*args, *after, *through)
     )
@@ -428,9 +430,10 @@
     return pl.BlockSpec((2,) + base.shape[1:], lambda i: (pair, 0, 0))
 
 
-def attend(ring, batches, lens, near, unit, weights, at, pair, after=()):
+def attend(ring, batches, lens, near, unit, weights, at, pair, us, after=()):
     rows, width = unit.shape
-    shapes = [out_of((rows, c * LANES), BF) for c in (2, 1, 1, 1)]
+    shapes = [pltpu.HBM((rows, c * LANES), BF) for c in (2, 1, 1)]
+    shapes.append(out_of((rows, LANES), BF))
     return call(
         functools.partial(attend_kernel, batches, len(weights)),
         shapes,
@@ -441,6 +444,7 @@
         out_specs=[fixed(s) for s in shapes],
         grid=(1,),
         scratch=[pltpu.VMEM((width, 3 * LANES), BF)],
+        us=us,
         mib=16,
         after=after,
     )
@@ -903,7 +907,17 @@
     after = helds
     for p in range(pairs):
         fwd.append(
-            attend(ring, batches, lens, near, unit, *qkvs[p], p, after=after)
+            attend(
+                ring,
+                batches,
+                lens,
+                near,
+                unit,
+                *qkvs[p],
+                p,
+                C2 if p == pairs - 1 else C1 if p == 1 else 0.001,
+                after=after,
+            )
         )
         if p == 0:
             held1, own2 = join(
@@ -911,12 +925,12 @@
             )
             got1 = ring.first(held1)
             got2 = ring.far(own2)
+            (held1,) = join([held1, got1], [(two, 0, 2 * units)])
+            got1 = ring.last(held1)
             after = [held1, *out_w]
         if p == min(1, pairs - 1):
-            z2 = tuple(2 + i for i in z)
-            plan = [(two, 0, 2 * units), (z2, 0, 2 * units)]
-            held1, held2 = join([held1, got1, own2, *got2], plan, after=[fwd[p][0]])
-            got1, got2 = ring.last(held1), ring.first(held2)
+            (held2,) = join([own2, *got2], [(z, 0, 2 * units)], after=[fwd[p][0]])
+            got2 = ring.first(held2)
             after = [held2]
     mixed = [f[3] for f in fwd]
     others = list(zip(*[ring.exchange(o) for o in mixed]))

time: 241 us -> 239 us (level)
  local copies, waits for them, and re-layouts: 29.9 us -> 23.9 us
  starting transfers between devices: 51 us -> 53.9 us
    unnamed x151 -> x133, local copies, waits for them, and re-layouts: 23.3 us -> 17.3 us
    pallas_call x27 -> x28, Pallas kernels: 130 us -> 131 us  [call(): pl.pallas_call(body, out_shape=list(outs) + [mark] + [out_of(t.shape, t.d...]
  transfers between devices with their start and end apart: 45 -> 45, of which waited for: 7 -> 8; matrix products, arithmetic and copies ran while one was open for 6% -> 6% of each run, Pallas kernels for 53% -> 54%
where the time goes in v2:
time: 239 us; the launch traced here: 235 us
  Pallas kernels  131 us (55%)
  starting transfers between devices  53.9 us (23%)
  local copies, waits for them, and re-layouts  23.9 us (10%)
  waiting for transfers between devices  14 us (6%)
  other arithmetic  10.6 us (4%)
    pallas_call x28, Pallas kernels, call(): pl.pallas_call(body, out_shape=list(outs) + [mark] + [out_of(t.shape, t.d...  131 us
    ppermute x12, starting transfers between devices, far_all(): lax.ppermute(a, 'dp', [(i, i ^ 4 * (step + 1)) for i in range(self.dp)])  19.1 us
    ppermute x15, starting transfers between devices, near(): return lax.ppermute(array, ('dp', 'mp'), pairs)  17.6 us
    unnamed x133, local copies, waits for them, and re-layouts  17.3 us
    ppermute x9, starting transfers between devices, far(): lax.ppermute(array, 'dp', [(i, i ^ 4 * step) for i in range(self.dp)])  15.2 us
    ppermute x15, waiting for transfers between devices, near(): return lax.ppermute(array, ('dp', 'mp'), pairs)  7.81 us
    convert_element_type x2, other arithmetic, sums_of(): return [sum((f[r].astype(F32) for f in fields)).astype(BF) for r in rows]  6.33 us
  transfers between devices with their start and end apart: 45, of which 8 were waited for; matrix products, arithmetic and copies ran while one was open for 6% of the time, Pallas kernels for 54%

profile of v2, /device:TPU:0, one launch (start us, length us, event | category | flops | bytes accessed | tf_op | source)
XLA Modules:
  0.0 235.3 jit_solution(14733835049623929587)
XLA Ops:
  3.2 3.0 %collective-permute-start = (bf16[1,48,1536]{2,1,0:T(8,128)(2,1)S(1)}, bf16[1,48,1536]{2,1,0:T(8,128)(2,1)S(1)}, u32[]{:S(2)}, u32[]{:S(2)}) collective-permute-start(bf16[1,48,1536]{2,1,0:T(8,128)(2,1)S(1)} %bitcast.37), channel_id=1, source_target_pairs={{0,8},{2,10},{4,12},{6,14},{8,0},{10,2},{12,4},{14,6},{16,24},{18,... | collective-permute-start | bytes 442376 | tf_op jit(solution)/shard_map/ppermute | solution.py:127
  6.3 2.6 %collective-permute-start.1 = (bf16[1,48,1536]{2,1,0:T(8,128)(2,1)S(1)}, bf16[1,48,1536]{2,1,0:T(8,128)(2,1)S(1)}, u32[]{:S(2)}, u32[]{:S(2)}) collective-permute-start(bf16[1,48,1536]{2,1,0:T(8,128)(2,1)S(1)} %bitcast.38), channel_id=1, source_target_pairs={{0,16},{2,18},{4,20},{6,22},{8,24},{10,26},{12,28},{14,30},{16,0},... | collective-permute-start | bytes 442376 | tf_op jit(solution)/shard_map/ppermute | solution.py:127
  10.8 4.0 %shard_map.255 = (bf16[6,128,1024]{2,1,0:T(8,128)(2,1)S(1)}, bf16[6,128,1024]{2,1,0:T(8,128)(2,1)S(1)}, f32[8,128]{1,0:T(8,128)S(1)}) custom-call(s32[15]{0:T(128)S(1)} %copy-done.57, bf16[8,32]{1,0:T(8,128)(2,1)S(1)} %pad.4.refs_1_, bf16[1,48,1536]{2,1,0:T(8,128)(2,1)S(1)} %bitcast.40), custom_call_target="tpu_custom_call" | custom-call | flops 1000000 | bytes 1000 | tf_op jit(solution)/shard_map/pallas_call | solution.py:82
  17.0 3.2 %collective-permute-done.1.refs_2_ = bf16[1,48,1536]{2,1,0:T(8,128)(2,1)S(1)} collective-permute-done((bf16[1,48,1536]{2,1,0:T(8,128)(2,1)S(1)}, bf16[1,48,1536]{2,1,0:T(8,128)(2,1)S(1)}, u32[]{:S(2)}, u32[]{:S(2)}) %collective-permute-start.1) | collective-permute-done | bytes 147488 | tf_op jit(solution)/shard_map/ppermute | solution.py:127
  25.4 4.9 %collective-permute-done.3.refs_1_ = bf16[4,48,1536]{2,1,0:T(8,128)(2,1)S(1)} collective-permute-done((bf16[4,48,1536]{2,1,0:T(8,128)(2,1)S(1)}, bf16[4,48,1536]{2,1,0:T(8,128)(2,1)S(1)}, u32[]{:S(2)}, u32[]{:S(2)}) %collective-permute-start.3) | collective-permute-done | bytes 589856 | tf_op jit(solution)/shard_map/ppermute | solution.py:143
  33.4 2.3 collective-permute-start.6
  39.8 7.6 %shard_map.259 = (bf16[2048,256]{1,0:T(8,128)(2,1)}, bf16[2048,128]{1,0:T(8,128)(2,1)}, bf16[2048,128]{1,0:T(8,128)(2,1)}, bf16[2048,128]{1,0:T(8,128)(2,1)}, f32[8,128]{1,0:T(8,128)S(1)}) custom-call(s32[17]{0:T(128)S(1)} %pad_add_fusion.refs_0_.refs_3_, s32[4]{0:T(128)S(1)} %copy-done.55, s32[2]{0:T(128)S(1)} %copy-done.56, ...), custom_call_target="tpu_custom_call" | custom-call | flops 1000000 | bytes 1000 | tf_op jit(solution)/shard_map/pallas_call | solution.py:82
  50.5 2.3 collective-permute-start.10
  56.3 2.6 %collective-permute-done.9.refs_1_ = bf16[4,48,1536]{2,1,0:T(8,128)(2,1)S(1)} collective-permute-done((bf16[4,48,1536]{2,1,0:T(8,128)(2,1)S(1)}, bf16[4,48,1536]{2,1,0:T(8,128)(2,1)S(1)}, u32[]{:S(2)}, u32[]{:S(2)}) %collective-permute-start.9) | collective-permute-done | bytes 589856 | tf_op jit(solution)/shard_map/ppermute | solution.py:143
  63.3 7.6 %shard_map.262 = (bf16[2048,256]{1,0:T(8,128)(2,1)}, bf16[2048,128]{1,0:T(8,128)(2,1)}, bf16[2048,128]{1,0:T(8,128)(2,1)}, bf16[2048,128]{1,0:T(8,128)(2,1)}, f32[8,128]{1,0:T(8,128)S(1)}) custom-call(s32[17]{0:T(128)S(1)} %pad_add_fusion.refs_0_.refs_3_, s32[4]{0:T(128)S(1)} %copy-done.55, s32[2]{0:T(128)S(1)} %copy-done.56, ...), custom_call_target="tpu_custom_call" | custom-call | flops 1500000000 | bytes 1000 | tf_op jit(solution)/shard_map/pallas_call | solution.py:82
  74.4 7.7 %shard_map.264 = (bf16[2048,256]{1,0:T(8,128)(2,1)}, bf16[2048,128]{1,0:T(8,128)(2,1)}, bf16[2048,128]{1,0:T(8,128)(2,1)}, bf16[2048,128]{1,0:T(8,128)(2,1)}, f32[8,128]{1,0:T(8,128)S(1)}) custom-call(s32[17]{0:T(128)S(1)} %pad_add_fusion.refs_0_.refs_3_, s32[4]{0:T(128)S(1)} %copy-done.55, s32[2]{0:T(128)S(1)} %copy-done.56, ...), custom_call_target="tpu_custom_call" | custom-call | flops 6000000000 | bytes 1000 | tf_op jit(solution)/shard_map/pallas_call | solution.py:82
  88.3 26.9 %shard_map.266 = (bf16[2048,768]{1,0:T(8,128)(2,1)}, f32[2048,128]{1,0:T(8,128)S(1)}, bf16[2048,768]{1,0:T(8,128)(2,1)}, bf16[2048,768]{1,0:T(8,128)(2,1)}, f32[...) custom-call(s32[17]{0:T(128)S(1)} %pad_add_fusion.refs_0_.refs_3_, s32[16]{0:T(128)S(1)} %fusion.3.refs_1_, ...), custom_call_target="tpu_custom_call" | custom-call | flops 1000000 | bytes 1000 | tf_op jit(solution)/shard_map/pallas_call | solution.py:82
  116.4 15.7 %shard_map.267 = (bf16[2048,768]{1,0:T(8,128)(2,1)}, bf16[2048,768]{1,0:T(8,128)(2,1)S(1)}, bf16[2048,768]{1,0:T(8,128)(2,1)}, bf16[2048,768]{1,0:T(8,128)(2,1)}, f32[8,128]{1,0:T(8,128)}) custom-call(s32[17]{0:T(128)S(1)} %pad_add_fusion.refs_0_.refs_3_, bf16[2048,768]{1,0:T(8,128)(2,1)} %get-tuple-element.149.refs_1_, ...), custom_call_target="tpu_custom_call" | custom-call | flops 1000000 | bytes 1000 | tf_op jit(solution)/shard_map/pallas_call | solution.py:82
  137.6 7.0 %shard_map.269 = (f32[8,48,1536]{2,1,0:T(8,128)S(1)}, bf16[8,48,1536]{2,1,0:T(8,128)(2,1)S(1)}, f32[8,128]{1,0:T(8,128)S(1)}) custom-call(s32[17]{0:T(128)S(1)} %pad_add_fusion.refs_0_.refs_3_, bf16[2048,768]{1,0:T(8,128)(2,1)S(1)} %copy-done.8, bf16[1024,768]{1,0:T(8,128)(2,1)S(1)} %bitcast.23, bf16[1024,768]{1,0:T(8,128)(2,1)S(1)} %bitcast.26, ...), custom_call_target="tpu_custom_call" | custom-call | flops 1000000 | bytes 1000 | tf_op jit(solution)/shard_map/pallas_call | solution.py:82
  146.4 6.9 %shard_map.271 = (bf16[2048,384]{1,0:T(8,128)(2,1)S(1)}, f32[768,384]{1,0:T(8,128)S(1)}, f32[8,128]{1,0:T(8,128)}) custom-call(s32[17]{0:T(128)S(1)} %pad_add_fusion.refs_0_.refs_3_, bf16[2048,768]{1,0:T(8,128)(2,1)S(1)} %get-tuple-element.156.refs_1_.refs_3_, bf16[2048,768]{1,0:T(8,128)(2,1)S(1)} %collective-permute-done.22.refs_2_.refs_4_, ...), custom_call_target="tpu_custom_call" | custom-call | flops 1000000 | bytes 1000 | tf_op jit(solution)/shard_map/pallas_call | solution.py:82
  153.4 8.7 %shard_map.272 = (bf16[2048,384]{1,0:T(8,128)(2,1)S(1)}, f32[8,128]{1,0:T(8,128)S(1)}, f32[768,384]{1,0:T(8,128)S(1)}, f32[8,128]{1,0:T(8,128)S(1)}) custom-call(s32[4]{0:T(128)S(1)} %copy-done.55, s32[2]{0:T(128)S(1)} %copy-done.56, s32[15]{0:T(128)S(1)} %copy-done.58, s32[17]{0:T(128)S(1)} %pad_add_fusion.refs_0_.refs_3_, ...), custom_call_target="tpu_custom_call" | custom-call | flops 1000000 | bytes 1000 | tf_op jit(solution)/shard_map/pallas_call | solution.py:82
  163.9 2.3 collective-permute-start.26
  168.7 9.1 %shard_map.274 = (bf16[2048,384]{1,0:T(8,128)(2,1)S(1)}, f32[8,128]{1,0:T(8,128)S(1)}, f32[8,48,1152]{2,1,0:T(8,128)S(1)}, bf16[8,48,1152]{2,1,0:T(8,128)(2,1)S(1)}, f32[8,128]{1,0:T(8,128)S(1)}) custom-call(s32[4]{0:T(128)S(1)} %copy-done.55, s32[2]{0:T(128)S(1)} %copy-done.56, s32[15]{0:T(128)S(1)} %copy-done.58, s32[17]{0:T(128)S(1)} %pad_add_fusion.refs_0_.refs_3_, ...), custom_call_target="tpu_custom_call" | custom-call | flops 1000000 | bytes 1000 | tf_op jit(solution)/shard_map/pallas_call | solution.py:82
  181.5 2.1 collective-permute-start.30
  186.0 9.4 %shard_map.276 = (bf16[2048,384]{1,0:T(8,128)(2,1)S(1)}, f32[8,128]{1,0:T(8,128)}, f32[8,48,512]{2,1,0:T(8,128)S(1)}, bf16[8,48,512]{2,1,0:T(8,128)(2,1)S(1)}, f32[8,128]{1,0:T(8,128)}) custom-call(s32[4]{0:T(128)S(1)} %copy-done.55, s32[2]{0:T(128)S(1)} %copy-done.56, s32[15]{0:T(128)S(1)} %copy-done.58, s32[17]{0:T(128)S(1)} %pad_add_fusion.refs_0_.refs_3_, ...), custom_call_target="tpu_custom_call" | custom-call | flops 1000000 | bytes 1000 | tf_op jit(solution)/shard_map/pallas_call | solution.py:82
  199.1 9.0 %shard_map.278 = (bf16[2048,768]{1,0:T(8,128)(2,1)S(1)}, f32[8,128]{1,0:T(8,128)}) custom-call(s32[17]{0:T(128)S(1)} %pad_add_fusion.refs_0_.refs_3_, bf16[1024,768]{1,0:T(8,128)(2,1)S(1)} %bitcast.29, bf16[1024,768]{1,0:T(8,128)(2,1)S(1)} %bitcast.32, bf16[2048,768]{1,0:T(8,128)(2,1)S(1)} %get-tuple-element.156.refs_1_.refs_3_, ...), custom_call_target="tpu_custom_call" | custom-call | flops 1000000 | bytes 1000 | tf_op jit(solution)/shard_map/pallas_call | solution.py:82
  211.5 2.1 collective-permute-start.38
  222.4 3.6 %add_convert_fusion.2 = (bf16[1024,768]{1,0:T(8,128)(2,1)S(1)}, bf16[1024,768]{1,0:T(8,128)(2,1)S(1)}) fusion(bf16[2048,768]{1,0:T(8,128)(2,1)} %collective-permute-done.36, bf16[2048,768]{1,0:T(8,128)(2,1)} %get-tuple-element.212), kind=kLoop, calls=%fused_computation.2 | loop fusion | flops 6291456 | bytes 9437184 | tf_op jit(solution)/shard_map/convert_element_type | solution.py:1004
  227.6 2.7 %add_convert_fusion = (bf16[1024,768]{1,0:T(8,128)(2,1)S(1)}, bf16[1024,768]{1,0:T(8,128)(2,1)S(1)}) fusion(bf16[2048,768]{1,0:T(8,128)(2,1)} %collective-permute-done.37, bf16[2048,768]{1,0:T(8,128)(2,1)S(1)} %get-tuple-element.213), kind=kLoop, calls=%fused_computation | loop fusion | flops 6291456 | bytes 9437184 | tf_op jit(solution)/shard_map/convert_element_type | solution.py:1004
  (249 shorter events, 80.2 us)
Async XLA Ops:
  3.2 13.8 %collective-permute-start = (bf16[1,48,1536]{2,1,0:T(8,128)(2,1)S(1)}, bf16[1,48,1536]{2,1,0:T(8,128)(2,1)S(1)}, u32[]{:S(2)}, u32[]{:S(2)}) collective-permute-start(bf16[1,48,1536]{2,1,0:T(8,128)(2,1)S(1)} %bitcast.37), channel_id=1, source_target_pairs={{0,8},{2,10},{4,12},{6,14},{8,0},{10,2},{12,4},{14,6},{16,24},{18,... | collective-permute-start | bytes 442376 | tf_op jit(solution)/shard_map/ppermute | solution.py:127
  6.3 14.0 %collective-permute-start.1 = (bf16[1,48,1536]{2,1,0:T(8,128)(2,1)S(1)}, bf16[1,48,1536]{2,1,0:T(8,128)(2,1)S(1)}, u32[]{:S(2)}, u32[]{:S(2)}) collective-permute-start(bf16[1,48,1536]{2,1,0:T(8,128)(2,1)S(1)} %bitcast.38), channel_id=1, source_target_pairs={{0,16},{2,18},{4,20},{6,22},{8,24},{10,26},{12,28},{14,30},{16,0},... | collective-permute-start | bytes 442376 | tf_op jit(solution)/shard_map/ppermute | solution.py:127
  32.9 27.1 %collective-permute-start.5 = (bf16[8,48,1152]{2,1,0:T(8,128)(2,1)}, bf16[8,48,1152]{2,1,0:T(8,128)(2,1)}, u32[]{:S(2)}, u32[]{:S(2)}) collective-permute-start(bf16[8,48,1152]{2,1,0:T(8,128)(2,1)} %get-tuple-element.132.refs_5_.refs_10_), channel_id=1, source_target_pairs={{0,4},{1,3},{2,6},{3,1},{4,0},{5,7},{6,2},{7,5},{8,12},{9,11},{10,... | collective-permute-start | bytes 2654216 | tf_op jit(solution)/shard_map/ppermute | solution.py:143
  33.4 14.0 %collective-permute-start.6 = (bf16[1,48,1536]{2,1,0:T(8,128)(2,1)S(1)}, bf16[1,48,1536]{2,1,0:T(8,128)(2,1)S(1)}, u32[]{:S(2)}, u32[]{:S(2)}) collective-permute-start(bf16[1,48,1536]{2,1,0:T(8,128)(2,1)S(1)} %get-tuple-element.133.refs_0_), channel_id=1, source_target_pairs={{0,8},{2,10},{4,12},{6,14},{8,0},{10,2},{12,4},{14,6},{16,24},{18,... | collective-permute-start | bytes 442376 | tf_op jit(solution)/shard_map/ppermute | solution.py:127
  50.5 20.3 %collective-permute-start.10 = (bf16[1,48,1536]{2,1,0:T(8,128)(2,1)}, bf16[1,48,1536]{2,1,0:T(8,128)(2,1)S(1)}, u32[]{:S(2)}, u32[]{:S(2)}) collective-permute-start(bf16[1,48,1536]{2,1,0:T(8,128)(2,1)} %get-tuple-element.139.refs_0_), channel_id=1, source_target_pairs={{0,8},{2,10},{4,12},{6,14},{8,0},{10,2},{12,4},{14,6},{16,24},{18,... | collective-permute-start | bytes 442376 | tf_op jit(solution)/shard_map/ppermute | solution.py:127
  52.8 18.3 %collective-permute-start.11 = (bf16[1,48,1536]{2,1,0:T(8,128)(2,1)}, bf16[1,48,1536]{2,1,0:T(8,128)(2,1)S(1)}, u32[]{:S(2)}, u32[]{:S(2)}) collective-permute-start(bf16[1,48,1536]{2,1,0:T(8,128)(2,1)} %get-tuple-element.139.refs_0_), channel_id=1, source_target_pairs={{0,16},{2,18},{4,20},{6,22},{8,24},{10,26},{12,28},{14,30},{16,0},... | collective-permute-start | bytes 442376 | tf_op jit(solution)/shard_map/ppermute | solution.py:127
  53.9 18.0 %collective-permute-start.12 = (bf16[1,48,1536]{2,1,0:T(8,128)(2,1)}, bf16[1,48,1536]{2,1,0:T(8,128)(2,1)S(1)}, u32[]{:S(2)}, u32[]{:S(2)}) collective-permute-start(bf16[1,48,1536]{2,1,0:T(8,128)(2,1)} %get-tuple-element.139.refs_0_), channel_id=1, source_target_pairs={{0,24},{2,26},{4,28},{6,30},{8,16},{10,18},{12,20},{14,22},{16,8},... | collective-permute-start | bytes 442376 | tf_op jit(solution)/shard_map/ppermute | solution.py:127
  58.9 23.1 %collective-permute-start.17 = (bf16[8,48,384]{2,1,0:T(8,128)(2,1)S(1)}, bf16[8,48,384]{2,1,0:T(8,128)(2,1)S(1)}, u32[]{:S(2)}, u32[]{:S(2)}) collective-permute-start(bf16[8,48,384]{2,1,0:T(8,128)(2,1)S(1)} %slice.91.refs_8_.refs_14_.refs_6_), channel_id=1, source_target_pairs={{0,1},{1,0},{2,3},{3,2},{4,5},{5,4},{6,7},{7,6},{8,9},{9,8},{10,11... | collective-permute-start | bytes 884744 | tf_op jit(solution)/shard_map/ppermute | solution.py:153
  60.0 27.3 %collective-permute-start.16 = (bf16[8,48,1536]{2,1,0:T(8,128)(2,1)}, bf16[8,48,1536]{2,1,0:T(8,128)(2,1)}, u32[]{:S(2)}, u32[]{:S(2)}) collective-permute-start(bf16[8,48,1536]{2,1,0:T(8,128)(2,1)} %get-tuple-element.143.refs_12_), channel_id=1, source_target_pairs={{0,4},{1,3},{2,6},{3,1},{4,0},{5,7},{6,2},{7,5},{8,12},{9,11},{10,... | collective-permute-start | bytes 3538952 | tf_op jit(solution)/shard_map/ppermute | solution.py:143
  70.9 15.4 %collective-permute-start.13 = (bf16[2048,128]{1,0:T(8,128)(2,1)}, bf16[2048,128]{1,0:T(8,128)(2,1)}, u32[]{:S(2)}, u32[]{:S(2)}) collective-permute-start(bf16[2048,128]{1,0:T(8,128)(2,1)} %get-tuple-element.131.refs_6_.refs_3_.refs_9_), channel_id=1, source_target_pairs={{0,1},{1,0},{2,3},{3,2},{4,5},{5,4},{6,7},{7,6},{8,9},{9,8},{10,11... | collective-permute-start | bytes 1572872 | tf_op jit(solution)/shard_map/ppermute | solution.py:153
  71.1 16.2 %collective-permute-start.14 = (bf16[2048,128]{1,0:T(8,128)(2,1)}, bf16[2048,128]{1,0:T(8,128)(2,1)}, u32[]{:S(2)}, u32[]{:S(2)}) collective-permute-start(bf16[2048,128]{1,0:T(8,128)(2,1)} %get-tuple-element.138.refs_7_.refs_4_.refs_9_), channel_id=1, source_target_pairs={{0,1},{1,0},{2,3},{3,2},{4,5},{5,4},{6,7},{7,6},{8,9},{9,8},{10,11... | collective-permute-start | bytes 1572872 | tf_op jit(solution)/shard_map/ppermute | solution.py:153
  86.3 30.1 %collective-permute-start.21 = (bf16[8,48,1536]{2,1,0:T(8,128)(2,1)S(1)}, bf16[8,48,1536]{2,1,0:T(8,128)(2,1)S(1)}, u32[]{:S(2)}, u32[]{:S(2)}) collective-permute-start(bf16[8,48,1536]{2,1,0:T(8,128)(2,1)S(1)} %get-tuple-element.153.refs_7_), channel_id=1, source_target_pairs={{0,4},{1,3},{2,6},{3,1},{4,0},{5,7},{6,2},{7,5},{8,12},{9,11},{10,... | collective-permute-start | bytes 3538952 | tf_op jit(solution)/shard_map/ppermute | solution.py:143
  115.2 16.9 %collective-permute-start.20 = (bf16[8,48,1536]{2,1,0:T(8,128)(2,1)S(1)}, bf16[8,48,1536]{2,1,0:T(8,128)(2,1)S(1)}, u32[]{:S(2)}, u32[]{:S(2)}) collective-permute-start(bf16[8,48,1536]{2,1,0:T(8,128)(2,1)S(1)} %get-tuple-element.148), channel_id=1, source_target_pairs={{0,4},{1,3},{2,6},{3,1},{4,0},{5,7},{6,2},{7,5},{8,12},{9,11},{10,... | collective-permute-start | bytes 3538952 | tf_op jit(solution)/shard_map/ppermute | solution.py:143
  145.4 16.7 %collective-permute-start.24 = (bf16[8,48,1536]{2,1,0:T(8,128)(2,1)S(1)}, bf16[8,48,1536]{2,1,0:T(8,128)(2,1)S(1)}, u32[]{:S(2)}, u32[]{:S(2)}) collective-permute-start(bf16[8,48,1536]{2,1,0:T(8,128)(2,1)S(1)} %get-tuple-element.177), channel_id=1, source_target_pairs={{0,4},{1,3},{2,6},{3,1},{4,0},{5,7},{6,2},{7,5},{8,12},{9,11},{10,... | collective-permute-start | bytes 3538952 | tf_op jit(solution)/shard_map/ppermute | solution.py:143
  162.4 17.2 %collective-permute-start.25 = (bf16[4,48,1536]{2,1,0:T(8,128)(2,1)S(1)}, bf16[4,48,1536]{2,1,0:T(8,128)(2,1)S(1)}, u32[]{:S(2)}, u32[]{:S(2)}) collective-permute-start(bf16[4,48,1536]{2,1,0:T(8,128)(2,1)S(1)} %get-tuple-element.182), channel_id=1, source_target_pairs={{0,2},{1,5},{2,0},{3,7},{4,6},{5,1},{6,4},{7,3},{8,10},{9,13},{10,... | collective-permute-start | bytes 1769480 | tf_op jit(solution)/shard_map/ppermute | solution.py:143
  163.9 14.0 %collective-permute-start.26 = (bf16[48,1536]{1,0:T(8,128)(2,1)S(1)}, bf16[48,1536]{1,0:T(8,128)(2,1)S(1)}, u32[]{:S(2)}, u32[]{:S(2)}) collective-permute-start(bf16[48,1536]{1,0:T(8,128)(2,1)S(1)} %get-tuple-element.184), channel_id=1, source_target_pairs={{0,8},{2,10},{4,12},{6,14},{8,0},{10,2},{12,4},{14,6},{16,24},{18,... | collective-permute-start | bytes 442376 | tf_op jit(solution)/shard_map/ppermute | solution.py:133
  166.2 13.4 %collective-permute-start.27 = (bf16[48,1536]{1,0:T(8,128)(2,1)S(1)}, bf16[48,1536]{1,0:T(8,128)(2,1)S(1)}, u32[]{:S(2)}, u32[]{:S(2)}) collective-permute-start(bf16[48,1536]{1,0:T(8,128)(2,1)S(1)} %get-tuple-element.185), channel_id=1, source_target_pairs={{0,16},{2,18},{4,20},{6,22},{8,24},{10,26},{12,28},{14,30},{16,0},... | collective-permute-start | bytes 442376 | tf_op jit(solution)/shard_map/ppermute | solution.py:133
  180.5 15.6 %collective-permute-start.29 = (bf16[8,48,1152]{2,1,0:T(8,128)(2,1)S(1)}, bf16[8,48,1152]{2,1,0:T(8,128)(2,1)S(1)}, u32[]{:S(2)}, u32[]{:S(2)}) collective-permute-start(bf16[8,48,1152]{2,1,0:T(8,128)(2,1)S(1)} %get-tuple-element.188), channel_id=1, source_target_pairs={{0,4},{1,3},{2,6},{3,1},{4,0},{5,7},{6,2},{7,5},{8,12},{9,11},{10,... | collective-permute-start | bytes 2654216 | tf_op jit(solution)/shard_map/ppermute | solution.py:143
  181.5 14.0 %collective-permute-start.30 = (bf16[48,1536]{1,0:T(8,128)(2,1)S(1)}, bf16[48,1536]{1,0:T(8,128)(2,1)S(1)}, u32[]{:S(2)}, u32[]{:S(2)}) collective-permute-start(bf16[48,1536]{1,0:T(8,128)(2,1)S(1)} %get-tuple-element.189), channel_id=1, source_target_pairs={{0,8},{2,10},{4,12},{6,14},{8,0},{10,2},{12,4},{14,6},{16,24},{18,... | collective-permute-start | bytes 442376 | tf_op jit(solution)/shard_map/ppermute | solution.py:133
  199.0 16.2 %collective-permute-start.36 = (bf16[2048,768]{1,0:T(8,128)(2,1)}, bf16[2048,768]{1,0:T(8,128)(2,1)}, u32[]{:S(2)}, u32[]{:S(2)}) collective-permute-start(bf16[2048,768]{1,0:T(8,128)(2,1)} %get-tuple-element.211.refs_4_), channel_id=1, source_target_pairs={{0,1},{1,0},{2,3},{3,2},{4,5},{5,4},{6,7},{7,6},{8,9},{9,8},{10,11... | collective-permute-start | bytes 9437192 | tf_op jit(solution)/shard_map/ppermute | solution.py:153
  211.5 14.4 %collective-permute-start.38 = (bf16[48,1152]{1,0:T(8,128)(2,1)}, bf16[48,1152]{1,0:T(8,128)(2,1)S(1)}, u32[]{:S(2)}, u32[]{:S(2)}) collective-permute-start(bf16[48,1152]{1,0:T(8,128)(2,1)} %copy-done.61), channel_id=1, source_target_pairs={{0,8},{2,10},{4,12},{6,14},{8,0},{10,2},{12,4},{14,6},{16,24},{18,... | collective-permute-start | bytes 331784 | tf_op jit(solution)/shard_map/ppermute | solution.py:133
  213.6 18.6 %collective-permute-start.39 = (bf16[48,1152]{1,0:T(8,128)(2,1)}, bf16[48,1152]{1,0:T(8,128)(2,1)S(1)}, u32[]{:S(2)}, u32[]{:S(2)}) collective-permute-start(bf16[48,1152]{1,0:T(8,128)(2,1)} %copy-done.60), channel_id=1, source_target_pairs={{0,16},{2,18},{4,20},{6,22},{8,24},{10,26},{12,28},{14,30},{16,0},... | collective-permute-start | bytes 331784 | tf_op jit(solution)/shard_map/ppermute | solution.py:133
  215.2 16.9 %collective-permute-start.40 = (bf16[48,1152]{1,0:T(8,128)(2,1)}, bf16[48,1152]{1,0:T(8,128)(2,1)S(1)}, u32[]{:S(2)}, u32[]{:S(2)}) collective-permute-start(bf16[48,1152]{1,0:T(8,128)(2,1)} %copy-done.59), channel_id=1, source_target_pairs={{0,24},{2,26},{4,28},{6,30},{8,16},{10,18},{12,20},{14,22},{16,8},... | collective-permute-start | bytes 331784 | tf_op jit(solution)/shard_map/ppermute | solution.py:133
  219.3 12.9 %collective-permute-start.41 = (bf16[48,512]{1,0:T(8,128)(2,1)S(1)}, bf16[48,512]{1,0:T(8,128)(2,1)S(1)}, u32[]{:S(2)}, u32[]{:S(2)}) collective-permute-start(bf16[48,512]{1,0:T(8,128)(2,1)S(1)} %get-tuple-element.222), channel_id=1, source_target_pairs={{0,8},{2,10},{4,12},{6,14},{8,0},{10,2},{12,4},{14,6},{16,24},{18,... | collective-permute-start | bytes 147464 | tf_op jit(solution)/shard_map/ppermute | solution.py:133
  (83 other events, 514.5 us)

commit v3 on v2

--- a/solution.py
+++ b/solution.py
@@ -445,7 +445,7 @@
         grid=(1,),
         scratch=[pltpu.VMEM((width, 3 * LANES), BF)],
         us=us,
-        mib=16,
+        mib=14,
         after=after,
     )
 
@@ -547,7 +547,7 @@
             pltpu.VMEM((2,) + far.shape[1:], F32),
             pltpu.VMEM((8, LANES) if given else (width, cols), F32),
         ],
-        mib=24,
+        mib=20,
         after=after,
     )
     if not given:
@@ -754,7 +754,7 @@
         out_specs=[fixed(o) for o in outs],
         grid=(rows // tile,),
         scratch=[pltpu.VMEM((width, cols), F32)],
-        mib=32,
+        mib=26,
         after=after,
     )
 
@@ -790,7 +790,7 @@
         out_specs=[tiles(go, tile), fixed(total)],
         grid=(rows // tile,),
         scratch=[pltpu.VMEM((width, cols), BF)],
-        mib=24,
+        mib=20,
         after=after,
     )
 
@@ -829,7 +829,7 @@
         out_specs=[tiles(out, tile)],
         grid=(rows // tile,),
         scratch=[pltpu.VMEM((width, 3 * pairs * LANES), BF)],
-        mib=20,
+        mib=16,
         after=after,
     )[0]
 

time: 239 us -> 236 us (0.987)
  local copies, waits for them, and re-layouts: 23.9 us -> 21.5 us
    unnamed x133 -> x129, local copies, waits for them, and re-layouts: 17.3 us -> 14.9 us
  transfers between devices with their start and end apart: 45 -> 45, of which waited for: 8 -> 8; matrix products, arithmetic and copies ran while one was open for 6% -> 6% of each run, Pallas kernels for 54% -> 55%
where the time goes in v3:
time: 236 us; the launch traced here: 232 us
  Pallas kernels  130 us (55%)
  starting transfers between devices  53.8 us (23%)
  local copies, waits for them, and re-layouts  21.5 us (9%)
  waiting for transfers between devices  14.5 us (6%)
  other arithmetic  10.6 us (4%)
    pallas_call x28, Pallas kernels, call(): pl.pallas_call(body, out_shape=list(outs) + [mark] + [out_of(t.shape, t.d...  130 us
    ppermute x12, starting transfers between devices, far_all(): lax.ppermute(a, 'dp', [(i, i ^ 4 * (step + 1)) for i in range(self.dp)])  19.1 us
    ppermute x15, starting transfers between devices, near(): return lax.ppermute(array, ('dp', 'mp'), pairs)  17.6 us
    ppermute x9, starting transfers between devices, far(): lax.ppermute(array, 'dp', [(i, i ^ 4 * step) for i in range(self.dp)])  15.2 us
    unnamed x129, local copies, waits for them, and re-layouts  14.9 us
    ppermute x15, waiting for transfers between devices, near(): return lax.ppermute(array, ('dp', 'mp'), pairs)  8.2 us
    convert_element_type x2, other arithmetic, sums_of(): return [sum((f[r].astype(F32) for f in fields)).astype(BF) for r in rows]  6.33 us
  transfers between devices with their start and end apart: 45, of which 8 were waited for; matrix products, arithmetic and copies ran while one was open for 6% of the time, Pallas kernels for 55%

profile of v3, /device:TPU:0, one launch (start us, length us, event | category | flops | bytes accessed | tf_op | source)
XLA Modules:
  0.0 232.2 jit_solution(15133294487510668391)
XLA Ops:
  3.2 3.0 %collective-permute-start = (bf16[1,48,1536]{2,1,0:T(8,128)(2,1)S(1)}, bf16[1,48,1536]{2,1,0:T(8,128)(2,1)S(1)}, u32[]{:S(2)}, u32[]{:S(2)}) collective-permute-start(bf16[1,48,1536]{2,1,0:T(8,128)(2,1)S(1)} %bitcast.37), channel_id=1, source_target_pairs={{0,8},{2,10},{4,12},{6,14},{8,0},{10,2},{12,4},{14,6},{16,24},{18,... | collective-permute-start | bytes 442376 | tf_op jit(solution)/shard_map/ppermute | solution.py:127
  6.3 2.6 %collective-permute-start.1 = (bf16[1,48,1536]{2,1,0:T(8,128)(2,1)S(1)}, bf16[1,48,1536]{2,1,0:T(8,128)(2,1)S(1)}, u32[]{:S(2)}, u32[]{:S(2)}) collective-permute-start(bf16[1,48,1536]{2,1,0:T(8,128)(2,1)S(1)} %bitcast.38), channel_id=1, source_target_pairs={{0,16},{2,18},{4,20},{6,22},{8,24},{10,26},{12,28},{14,30},{16,0},... | collective-permute-start | bytes 442376 | tf_op jit(solution)/shard_map/ppermute | solution.py:127
  10.8 4.0 %shard_map.255 = (bf16[6,128,1024]{2,1,0:T(8,128)(2,1)S(1)}, bf16[6,128,1024]{2,1,0:T(8,128)(2,1)S(1)}, f32[8,128]{1,0:T(8,128)S(1)}) custom-call(s32[15]{0:T(128)S(1)} %copy-done.55, bf16[8,32]{1,0:T(8,128)(2,1)S(1)} %pad.4.refs_1_, bf16[1,48,1536]{2,1,0:T(8,128)(2,1)S(1)} %bitcast.40), custom_call_target="tpu_custom_call" | custom-call | flops 1000000 | bytes 1000 | tf_op jit(solution)/shard_map/pallas_call | solution.py:82
  17.0 3.2 %collective-permute-done.1.refs_2_ = bf16[1,48,1536]{2,1,0:T(8,128)(2,1)S(1)} collective-permute-done((bf16[1,48,1536]{2,1,0:T(8,128)(2,1)S(1)}, bf16[1,48,1536]{2,1,0:T(8,128)(2,1)S(1)}, u32[]{:S(2)}, u32[]{:S(2)}) %collective-permute-start.1) | collective-permute-done | bytes 147488 | tf_op jit(solution)/shard_map/ppermute | solution.py:127
  25.4 4.9 %collective-permute-done.3.refs_1_ = bf16[4,48,1536]{2,1,0:T(8,128)(2,1)S(1)} collective-permute-done((bf16[4,48,1536]{2,1,0:T(8,128)(2,1)S(1)}, bf16[4,48,1536]{2,1,0:T(8,128)(2,1)S(1)}, u32[]{:S(2)}, u32[]{:S(2)}) %collective-permute-start.3) | collective-permute-done | bytes 589856 | tf_op jit(solution)/shard_map/ppermute | solution.py:143
  33.4 2.3 collective-permute-start.6
  39.8 7.6 %shard_map.259 = (bf16[2048,256]{1,0:T(8,128)(2,1)}, bf16[2048,128]{1,0:T(8,128)(2,1)}, bf16[2048,128]{1,0:T(8,128)(2,1)}, bf16[2048,128]{1,0:T(8,128)(2,1)}, f32[8,128]{1,0:T(8,128)S(1)}) custom-call(s32[17]{0:T(128)S(1)} %pad_add_fusion.refs_0_.refs_3_, s32[4]{0:T(128)S(1)} %copy-done.53, s32[2]{0:T(128)S(1)} %copy-done.54, ...), custom_call_target="tpu_custom_call" | custom-call | flops 1000000 | bytes 1000 | tf_op jit(solution)/shard_map/pallas_call | solution.py:82
  50.5 2.3 collective-permute-start.10
  56.3 2.6 %collective-permute-done.9.refs_1_ = bf16[4,48,1536]{2,1,0:T(8,128)(2,1)S(1)} collective-permute-done((bf16[4,48,1536]{2,1,0:T(8,128)(2,1)S(1)}, bf16[4,48,1536]{2,1,0:T(8,128)(2,1)S(1)}, u32[]{:S(2)}, u32[]{:S(2)}) %collective-permute-start.9) | collective-permute-done | bytes 589856 | tf_op jit(solution)/shard_map/ppermute | solution.py:143
  63.3 7.6 %shard_map.262 = (bf16[2048,256]{1,0:T(8,128)(2,1)}, bf16[2048,128]{1,0:T(8,128)(2,1)}, bf16[2048,128]{1,0:T(8,128)(2,1)}, bf16[2048,128]{1,0:T(8,128)(2,1)}, f32[8,128]{1,0:T(8,128)S(1)}) custom-call(s32[17]{0:T(128)S(1)} %pad_add_fusion.refs_0_.refs_3_, s32[4]{0:T(128)S(1)} %copy-done.53, s32[2]{0:T(128)S(1)} %copy-done.54, ...), custom_call_target="tpu_custom_call" | custom-call | flops 1500000000 | bytes 1000 | tf_op jit(solution)/shard_map/pallas_call | solution.py:82
  74.4 7.6 %shard_map.264 = (bf16[2048,256]{1,0:T(8,128)(2,1)}, bf16[2048,128]{1,0:T(8,128)(2,1)}, bf16[2048,128]{1,0:T(8,128)(2,1)}, bf16[2048,128]{1,0:T(8,128)(2,1)}, f32[8,128]{1,0:T(8,128)S(1)}) custom-call(s32[17]{0:T(128)S(1)} %pad_add_fusion.refs_0_.refs_3_, s32[4]{0:T(128)S(1)} %copy-done.53, s32[2]{0:T(128)S(1)} %copy-done.54, ...), custom_call_target="tpu_custom_call" | custom-call | flops 6000000000 | bytes 1000 | tf_op jit(solution)/shard_map/pallas_call | solution.py:82
  88.3 26.9 %shard_map.266 = (bf16[2048,768]{1,0:T(8,128)(2,1)}, f32[2048,128]{1,0:T(8,128)S(1)}, bf16[2048,768]{1,0:T(8,128)(2,1)}, bf16[2048,768]{1,0:T(8,128)(2,1)}, f32[...) custom-call(s32[17]{0:T(128)S(1)} %pad_add_fusion.refs_0_.refs_3_, s32[16]{0:T(128)S(1)} %fusion.3.refs_1_, ...), custom_call_target="tpu_custom_call" | custom-call | flops 1000000 | bytes 1000 | tf_op jit(solution)/shard_map/pallas_call | solution.py:82
  116.4 15.9 %shard_map.267 = (bf16[2048,768]{1,0:T(8,128)(2,1)}, bf16[2048,768]{1,0:T(8,128)(2,1)S(1)}, bf16[2048,768]{1,0:T(8,128)(2,1)}, bf16[2048,768]{1,0:T(8,128)(2,1)}, f32[8,128]{1,0:T(8,128)}) custom-call(s32[17]{0:T(128)S(1)} %pad_add_fusion.refs_0_.refs_3_, bf16[2048,768]{1,0:T(8,128)(2,1)} %get-tuple-element.149.refs_1_, ...), custom_call_target="tpu_custom_call" | custom-call | flops 1000000 | bytes 1000 | tf_op jit(solution)/shard_map/pallas_call | solution.py:82
  136.1 7.0 %shard_map.269 = (f32[8,48,1536]{2,1,0:T(8,128)S(1)}, bf16[8,48,1536]{2,1,0:T(8,128)(2,1)S(1)}, f32[8,128]{1,0:T(8,128)S(1)}) custom-call(s32[17]{0:T(128)S(1)} %pad_add_fusion.refs_0_.refs_3_, bf16[2048,768]{1,0:T(8,128)(2,1)S(1)} %copy-done.8, bf16[1024,768]{1,0:T(8,128)(2,1)S(1)} %bitcast.23, bf16[1024,768]{1,0:T(8,128)(2,1)S(1)} %bitcast.26, ...), custom_call_target="tpu_custom_call" | custom-call | flops 1000000 | bytes 1000 | tf_op jit(solution)/shard_map/pallas_call | solution.py:82
  144.3 6.0 %shard_map.271 = (bf16[2048,384]{1,0:T(8,128)(2,1)S(1)}, f32[768,384]{1,0:T(8,128)S(1)}, f32[8,128]{1,0:T(8,128)}) custom-call(s32[17]{0:T(128)S(1)} %pad_add_fusion.refs_0_.refs_3_, bf16[2048,768]{1,0:T(8,128)(2,1)S(1)} %get-tuple-element.156.refs_1_.refs_3_, bf16[2048,768]{1,0:T(8,128)(2,1)S(1)} %collective-permute-done.22.refs_2_.refs_4_, ...), custom_call_target="tpu_custom_call" | custom-call | flops 1000000 | bytes 1000 | tf_op jit(solution)/shard_map/pallas_call | solution.py:82
  150.3 8.7 %shard_map.272 = (bf16[2048,384]{1,0:T(8,128)(2,1)S(1)}, f32[8,128]{1,0:T(8,128)S(1)}, f32[768,384]{1,0:T(8,128)S(1)}, f32[8,128]{1,0:T(8,128)S(1)}) custom-call(s32[4]{0:T(128)S(1)} %copy-done.53, s32[2]{0:T(128)S(1)} %copy-done.54, s32[15]{0:T(128)S(1)} %copy-done.56, s32[17]{0:T(128)S(1)} %pad_add_fusion.refs_0_.refs_3_, ...), custom_call_target="tpu_custom_call" | custom-call | flops 1000000 | bytes 1000 | tf_op jit(solution)/shard_map/pallas_call | solution.py:82
  161.0 2.3 collective-permute-start.26
  165.8 9.2 %shard_map.274 = (bf16[2048,384]{1,0:T(8,128)(2,1)S(1)}, f32[8,128]{1,0:T(8,128)S(1)}, f32[8,48,1152]{2,1,0:T(8,128)S(1)}, bf16[8,48,1152]{2,1,0:T(8,128)(2,1)S(1)}, f32[8,128]{1,0:T(8,128)S(1)}) custom-call(s32[4]{0:T(128)S(1)} %copy-done.53, s32[2]{0:T(128)S(1)} %copy-done.54, s32[15]{0:T(128)S(1)} %copy-done.56, s32[17]{0:T(128)S(1)} %pad_add_fusion.refs_0_.refs_3_, ...), custom_call_target="tpu_custom_call" | custom-call | flops 1000000 | bytes 1000 | tf_op jit(solution)/shard_map/pallas_call | solution.py:82
  178.4 2.1 collective-permute-start.30
  182.9 9.2 %shard_map.276 = (bf16[2048,384]{1,0:T(8,128)(2,1)S(1)}, f32[8,128]{1,0:T(8,128)}, f32[8,48,512]{2,1,0:T(8,128)S(1)}, bf16[8,48,512]{2,1,0:T(8,128)(2,1)S(1)}, f32[8,128]{1,0:T(8,128)}) custom-call(s32[4]{0:T(128)S(1)} %copy-done.53, s32[2]{0:T(128)S(1)} %copy-done.54, s32[15]{0:T(128)S(1)} %copy-done.56, s32[17]{0:T(128)S(1)} %pad_add_fusion.refs_0_.refs_3_, ...), custom_call_target="tpu_custom_call" | custom-call | flops 1000000 | bytes 1000 | tf_op jit(solution)/shard_map/pallas_call | solution.py:82
  195.9 8.9 %shard_map.278 = (bf16[2048,768]{1,0:T(8,128)(2,1)S(1)}, f32[8,128]{1,0:T(8,128)}) custom-call(s32[17]{0:T(128)S(1)} %pad_add_fusion.refs_0_.refs_3_, bf16[1024,768]{1,0:T(8,128)(2,1)S(1)} %bitcast.29, bf16[1024,768]{1,0:T(8,128)(2,1)S(1)} %bitcast.32, bf16[2048,768]{1,0:T(8,128)(2,1)S(1)} %get-tuple-element.156.refs_1_.refs_3_, ...), custom_call_target="tpu_custom_call" | custom-call | flops 1000000 | bytes 1000 | tf_op jit(solution)/shard_map/pallas_call | solution.py:82
  216.1 2.1 collective-permute-start.41
  219.3 3.6 %add_convert_fusion.2 = (bf16[1024,768]{1,0:T(8,128)(2,1)S(1)}, bf16[1024,768]{1,0:T(8,128)(2,1)S(1)}) fusion(bf16[2048,768]{1,0:T(8,128)(2,1)} %collective-permute-done.36, bf16[2048,768]{1,0:T(8,128)(2,1)} %get-tuple-element.212), kind=kLoop, calls=%fused_computation.2 | loop fusion | flops 6291456 | bytes 9437184 | tf_op jit(solution)/shard_map/convert_element_type | solution.py:1004
  224.5 2.7 %add_convert_fusion = (bf16[1024,768]{1,0:T(8,128)(2,1)S(1)}, bf16[1024,768]{1,0:T(8,128)(2,1)S(1)}) fusion(bf16[2048,768]{1,0:T(8,128)(2,1)} %collective-permute-done.37, bf16[2048,768]{1,0:T(8,128)(2,1)S(1)} %get-tuple-element.213), kind=kLoop, calls=%fused_computation | loop fusion | flops 6291456 | bytes 9437184 | tf_op jit(solution)/shard_map/convert_element_type | solution.py:1004
  (245 shorter events, 78.2 us)
Async XLA Ops:
  3.2 13.8 %collective-permute-start = (bf16[1,48,1536]{2,1,0:T(8,128)(2,1)S(1)}, bf16[1,48,1536]{2,1,0:T(8,128)(2,1)S(1)}, u32[]{:S(2)}, u32[]{:S(2)}) collective-permute-start(bf16[1,48,1536]{2,1,0:T(8,128)(2,1)S(1)} %bitcast.37), channel_id=1, source_target_pairs={{0,8},{2,10},{4,12},{6,14},{8,0},{10,2},{12,4},{14,6},{16,24},{18,... | collective-permute-start | bytes 442376 | tf_op jit(solution)/shard_map/ppermute | solution.py:127
  6.3 14.0 %collective-permute-start.1 = (bf16[1,48,1536]{2,1,0:T(8,128)(2,1)S(1)}, bf16[1,48,1536]{2,1,0:T(8,128)(2,1)S(1)}, u32[]{:S(2)}, u32[]{:S(2)}) collective-permute-start(bf16[1,48,1536]{2,1,0:T(8,128)(2,1)S(1)} %bitcast.38), channel_id=1, source_target_pairs={{0,16},{2,18},{4,20},{6,22},{8,24},{10,26},{12,28},{14,30},{16,0},... | collective-permute-start | bytes 442376 | tf_op jit(solution)/shard_map/ppermute | solution.py:127
  32.9 27.1 %collective-permute-start.5 = (bf16[8,48,1152]{2,1,0:T(8,128)(2,1)}, bf16[8,48,1152]{2,1,0:T(8,128)(2,1)}, u32[]{:S(2)}, u32[]{:S(2)}) collective-permute-start(bf16[8,48,1152]{2,1,0:T(8,128)(2,1)} %get-tuple-element.132.refs_5_.refs_10_), channel_id=1, source_target_pairs={{0,4},{1,3},{2,6},{3,1},{4,0},{5,7},{6,2},{7,5},{8,12},{9,11},{10,... | collective-permute-start | bytes 2654216 | tf_op jit(solution)/shard_map/ppermute | solution.py:143
  33.4 14.0 %collective-permute-start.6 = (bf16[1,48,1536]{2,1,0:T(8,128)(2,1)S(1)}, bf16[1,48,1536]{2,1,0:T(8,128)(2,1)S(1)}, u32[]{:S(2)}, u32[]{:S(2)}) collective-permute-start(bf16[1,48,1536]{2,1,0:T(8,128)(2,1)S(1)} %get-tuple-element.133.refs_0_), channel_id=1, source_target_pairs={{0,8},{2,10},{4,12},{6,14},{8,0},{10,2},{12,4},{14,6},{16,24},{18,... | collective-permute-start | bytes 442376 | tf_op jit(solution)/shard_map/ppermute | solution.py:127
  50.5 20.3 %collective-permute-start.10 = (bf16[1,48,1536]{2,1,0:T(8,128)(2,1)}, bf16[1,48,1536]{2,1,0:T(8,128)(2,1)S(1)}, u32[]{:S(2)}, u32[]{:S(2)}) collective-permute-start(bf16[1,48,1536]{2,1,0:T(8,128)(2,1)} %get-tuple-element.139.refs_0_), channel_id=1, source_target_pairs={{0,8},{2,10},{4,12},{6,14},{8,0},{10,2},{12,4},{14,6},{16,24},{18,... | collective-permute-start | bytes 442376 | tf_op jit(solution)/shard_map/ppermute | solution.py:127
  52.8 18.3 %collective-permute-start.11 = (bf16[1,48,1536]{2,1,0:T(8,128)(2,1)}, bf16[1,48,1536]{2,1,0:T(8,128)(2,1)S(1)}, u32[]{:S(2)}, u32[]{:S(2)}) collective-permute-start(bf16[1,48,1536]{2,1,0:T(8,128)(2,1)} %get-tuple-element.139.refs_0_), channel_id=1, source_target_pairs={{0,16},{2,18},{4,20},{6,22},{8,24},{10,26},{12,28},{14,30},{16,0},... | collective-permute-start | bytes 442376 | tf_op jit(solution)/shard_map/ppermute | solution.py:127
  53.9 18.0 %collective-permute-start.12 = (bf16[1,48,1536]{2,1,0:T(8,128)(2,1)}, bf16[1,48,1536]{2,1,0:T(8,128)(2,1)S(1)}, u32[]{:S(2)}, u32[]{:S(2)}) collective-permute-start(bf16[1,48,1536]{2,1,0:T(8,128)(2,1)} %get-tuple-element.139.refs_0_), channel_id=1, source_target_pairs={{0,24},{2,26},{4,28},{6,30},{8,16},{10,18},{12,20},{14,22},{16,8},... | collective-permute-start | bytes 442376 | tf_op jit(solution)/shard_map/ppermute | solution.py:127
  58.9 23.1 %collective-permute-start.17 = (bf16[8,48,384]{2,1,0:T(8,128)(2,1)S(1)}, bf16[8,48,384]{2,1,0:T(8,128)(2,1)S(1)}, u32[]{:S(2)}, u32[]{:S(2)}) collective-permute-start(bf16[8,48,384]{2,1,0:T(8,128)(2,1)S(1)} %slice.91.refs_8_.refs_14_.refs_6_), channel_id=1, source_target_pairs={{0,1},{1,0},{2,3},{3,2},{4,5},{5,4},{6,7},{7,6},{8,9},{9,8},{10,11... | collective-permute-start | bytes 884744 | tf_op jit(solution)/shard_map/ppermute | solution.py:153
  60.0 27.3 %collective-permute-start.16 = (bf16[8,48,1536]{2,1,0:T(8,128)(2,1)}, bf16[8,48,1536]{2,1,0:T(8,128)(2,1)}, u32[]{:S(2)}, u32[]{:S(2)}) collective-permute-start(bf16[8,48,1536]{2,1,0:T(8,128)(2,1)} %get-tuple-element.143.refs_12_), channel_id=1, source_target_pairs={{0,4},{1,3},{2,6},{3,1},{4,0},{5,7},{6,2},{7,5},{8,12},{9,11},{10,... | collective-permute-start | bytes 3538952 | tf_op jit(solution)/shard_map/ppermute | solution.py:143
  70.9 15.4 %collective-permute-start.13 = (bf16[2048,128]{1,0:T(8,128)(2,1)}, bf16[2048,128]{1,0:T(8,128)(2,1)}, u32[]{:S(2)}, u32[]{:S(2)}) collective-permute-start(bf16[2048,128]{1,0:T(8,128)(2,1)} %get-tuple-element.131.refs_6_.refs_3_.refs_9_), channel_id=1, source_target_pairs={{0,1},{1,0},{2,3},{3,2},{4,5},{5,4},{6,7},{7,6},{8,9},{9,8},{10,11... | collective-permute-start | bytes 1572872 | tf_op jit(solution)/shard_map/ppermute | solution.py:153
  71.1 16.2 %collective-permute-start.14 = (bf16[2048,128]{1,0:T(8,128)(2,1)}, bf16[2048,128]{1,0:T(8,128)(2,1)}, u32[]{:S(2)}, u32[]{:S(2)}) collective-permute-start(bf16[2048,128]{1,0:T(8,128)(2,1)} %get-tuple-element.138.refs_7_.refs_4_.refs_9_), channel_id=1, source_target_pairs={{0,1},{1,0},{2,3},{3,2},{4,5},{5,4},{6,7},{7,6},{8,9},{9,8},{10,11... | collective-permute-start | bytes 1572872 | tf_op jit(solution)/shard_map/ppermute | solution.py:153
  86.3 30.1 %collective-permute-start.21 = (bf16[8,48,1536]{2,1,0:T(8,128)(2,1)S(1)}, bf16[8,48,1536]{2,1,0:T(8,128)(2,1)S(1)}, u32[]{:S(2)}, u32[]{:S(2)}) collective-permute-start(bf16[8,48,1536]{2,1,0:T(8,128)(2,1)S(1)} %get-tuple-element.153.refs_7_), channel_id=1, source_target_pairs={{0,4},{1,3},{2,6},{3,1},{4,0},{5,7},{6,2},{7,5},{8,12},{9,11},{10,... | collective-permute-start | bytes 3538952 | tf_op jit(solution)/shard_map/ppermute | solution.py:143
  115.2 17.1 %collective-permute-start.20 = (bf16[8,48,1536]{2,1,0:T(8,128)(2,1)S(1)}, bf16[8,48,1536]{2,1,0:T(8,128)(2,1)S(1)}, u32[]{:S(2)}, u32[]{:S(2)}) collective-permute-start(bf16[8,48,1536]{2,1,0:T(8,128)(2,1)S(1)} %get-tuple-element.148), channel_id=1, source_target_pairs={{0,4},{1,3},{2,6},{3,1},{4,0},{5,7},{6,2},{7,5},{8,12},{9,11},{10,... | collective-permute-start | bytes 3538952 | tf_op jit(solution)/shard_map/ppermute | solution.py:143
  143.3 16.3 %collective-permute-start.24 = (bf16[8,48,1536]{2,1,0:T(8,128)(2,1)S(1)}, bf16[8,48,1536]{2,1,0:T(8,128)(2,1)S(1)}, u32[]{:S(2)}, u32[]{:S(2)}) collective-permute-start(bf16[8,48,1536]{2,1,0:T(8,128)(2,1)S(1)} %get-tuple-element.177), channel_id=1, source_target_pairs={{0,4},{1,3},{2,6},{3,1},{4,0},{5,7},{6,2},{7,5},{8,12},{9,11},{10,... | collective-permute-start | bytes 3538952 | tf_op jit(solution)/shard_map/ppermute | solution.py:143
  159.8 16.8 %collective-permute-start.25 = (bf16[4,48,1536]{2,1,0:T(8,128)(2,1)S(1)}, bf16[4,48,1536]{2,1,0:T(8,128)(2,1)S(1)}, u32[]{:S(2)}, u32[]{:S(2)}) collective-permute-start(bf16[4,48,1536]{2,1,0:T(8,128)(2,1)S(1)} %get-tuple-element.182), channel_id=1, source_target_pairs={{0,2},{1,5},{2,0},{3,7},{4,6},{5,1},{6,4},{7,3},{8,10},{9,13},{10,... | collective-permute-start | bytes 1769480 | tf_op jit(solution)/shard_map/ppermute | solution.py:143
  161.0 14.0 %collective-permute-start.26 = (bf16[48,1536]{1,0:T(8,128)(2,1)S(1)}, bf16[48,1536]{1,0:T(8,128)(2,1)S(1)}, u32[]{:S(2)}, u32[]{:S(2)}) collective-permute-start(bf16[48,1536]{1,0:T(8,128)(2,1)S(1)} %get-tuple-element.184), channel_id=1, source_target_pairs={{0,8},{2,10},{4,12},{6,14},{8,0},{10,2},{12,4},{14,6},{16,24},{18,... | collective-permute-start | bytes 442376 | tf_op jit(solution)/shard_map/ppermute | solution.py:133
  163.3 13.3 %collective-permute-start.27 = (bf16[48,1536]{1,0:T(8,128)(2,1)S(1)}, bf16[48,1536]{1,0:T(8,128)(2,1)S(1)}, u32[]{:S(2)}, u32[]{:S(2)}) collective-permute-start(bf16[48,1536]{1,0:T(8,128)(2,1)S(1)} %get-tuple-element.185), channel_id=1, source_target_pairs={{0,16},{2,18},{4,20},{6,22},{8,24},{10,26},{12,28},{14,30},{16,0},... | collective-permute-start | bytes 442376 | tf_op jit(solution)/shard_map/ppermute | solution.py:133
  177.4 15.6 %collective-permute-start.29 = (bf16[8,48,1152]{2,1,0:T(8,128)(2,1)S(1)}, bf16[8,48,1152]{2,1,0:T(8,128)(2,1)S(1)}, u32[]{:S(2)}, u32[]{:S(2)}) collective-permute-start(bf16[8,48,1152]{2,1,0:T(8,128)(2,1)S(1)} %get-tuple-element.188), channel_id=1, source_target_pairs={{0,4},{1,3},{2,6},{3,1},{4,0},{5,7},{6,2},{7,5},{8,12},{9,11},{10,... | collective-permute-start | bytes 2654216 | tf_op jit(solution)/shard_map/ppermute | solution.py:143
  178.4 13.8 %collective-permute-start.30 = (bf16[48,1536]{1,0:T(8,128)(2,1)S(1)}, bf16[48,1536]{1,0:T(8,128)(2,1)S(1)}, u32[]{:S(2)}, u32[]{:S(2)}) collective-permute-start(bf16[48,1536]{1,0:T(8,128)(2,1)S(1)} %get-tuple-element.189), channel_id=1, source_target_pairs={{0,8},{2,10},{4,12},{6,14},{8,0},{10,2},{12,4},{14,6},{16,24},{18,... | collective-permute-start | bytes 442376 | tf_op jit(solution)/shard_map/ppermute | solution.py:133
  195.9 16.2 %collective-permute-start.36 = (bf16[2048,768]{1,0:T(8,128)(2,1)}, bf16[2048,768]{1,0:T(8,128)(2,1)}, u32[]{:S(2)}, u32[]{:S(2)}) collective-permute-start(bf16[2048,768]{1,0:T(8,128)(2,1)} %get-tuple-element.211.refs_4_), channel_id=1, source_target_pairs={{0,1},{1,0},{2,3},{3,2},{4,5},{5,4},{6,7},{7,6},{8,9},{9,8},{10,11... | collective-permute-start | bytes 9437192 | tf_op jit(solution)/shard_map/ppermute | solution.py:153
  208.6 14.3 %collective-permute-start.38 = (bf16[48,1152]{1,0:T(8,128)(2,1)}, bf16[48,1152]{1,0:T(8,128)(2,1)S(1)}, u32[]{:S(2)}, u32[]{:S(2)}) collective-permute-start(bf16[48,1152]{1,0:T(8,128)(2,1)} %copy-done.59), channel_id=1, source_target_pairs={{0,8},{2,10},{4,12},{6,14},{8,0},{10,2},{12,4},{14,6},{16,24},{18,... | collective-permute-start | bytes 331784 | tf_op jit(solution)/shard_map/ppermute | solution.py:133
  210.6 18.5 %collective-permute-start.39 = (bf16[48,1152]{1,0:T(8,128)(2,1)}, bf16[48,1152]{1,0:T(8,128)(2,1)S(1)}, u32[]{:S(2)}, u32[]{:S(2)}) collective-permute-start(bf16[48,1152]{1,0:T(8,128)(2,1)} %copy-done.58), channel_id=1, source_target_pairs={{0,16},{2,18},{4,20},{6,22},{8,24},{10,26},{12,28},{14,30},{16,0},... | collective-permute-start | bytes 331784 | tf_op jit(solution)/shard_map/ppermute | solution.py:133
  212.2 16.9 %collective-permute-start.40 = (bf16[48,1152]{1,0:T(8,128)(2,1)}, bf16[48,1152]{1,0:T(8,128)(2,1)S(1)}, u32[]{:S(2)}, u32[]{:S(2)}) collective-permute-start(bf16[48,1152]{1,0:T(8,128)(2,1)} %copy-done.57), channel_id=1, source_target_pairs={{0,24},{2,26},{4,28},{6,30},{8,16},{10,18},{12,20},{14,22},{16,8},... | collective-permute-start | bytes 331784 | tf_op jit(solution)/shard_map/ppermute | solution.py:133
  216.1 13.0 %collective-permute-start.41 = (bf16[48,512]{1,0:T(8,128)(2,1)S(1)}, bf16[48,512]{1,0:T(8,128)(2,1)S(1)}, u32[]{:S(2)}, u32[]{:S(2)}) collective-permute-start(bf16[48,512]{1,0:T(8,128)(2,1)S(1)} %get-tuple-element.222), channel_id=1, source_target_pairs={{0,8},{2,10},{4,12},{6,14},{8,0},{10,2},{12,4},{14,6},{16,24},{18,... | collective-permute-start | bytes 147464 | tf_op jit(solution)/shard_map/ppermute | solution.py:133
  (81 other events, 499.7 us)
